TPU v7x, 256 devices: a whole 4x4x8 slice. The times are simulated.
256 devices in a mesh: tm: 32 (over z_hi, y, core), rows: 8 (over z_lo, x).
Axes of the slice: x: 4, y: 4, z: 8 (z_hi: 4, z_lo: 2; z = z_hi * 2 + z_lo), core: 2. Of those that a mesh axis runs over, the one named last changes fastest.
Arguments:
- frames_in: bfloat16 [32, 48, 160, 256], P('tm', 'rows'), may hold values from -6 to 6
- grad_out: bfloat16 [32, 48, 160, 256], P('tm', 'rows'), may hold values from -6 to 6
- conv_weight: bfloat16 [2, 9, 256, 256], replicated, may hold values from -0.125 to 0.125
- attn_weight: bfloat16 [4, 256, 256], replicated, may hold values from -0.375 to 0.375
Outputs:
- input_grad: bfloat16 [32, 48, 160, 256], P('tm', 'rows')
- conv_grad: float32 [2, 9, 256, 256], P(None, None, 'tm')
- attn_grad: float32 [4, 256, 256], P(None, 'tm')
All inputs are finite; a program needn't handle non-finite values.
Results may differ from a plain program's by a relative error of at most 0.027.
Values may be sent and summed in bfloat16 or wider, within the bound.
A program may use at most 64 MiB of HBM per device.

v0:
```python
import jax
import jax.numpy as jnp
from jax import lax
from jax.sharding import PartitionSpec as P

HEADS = 4


EPSILON = 1e-06


def extended(value, sides, width):
    for axis, dim in sides:
        size, length = (lax.axis_size(axis), value.shape[dim])
        up = [(i, (i + 1) % size) for i in range(size - 1)]
        down = [(j, i) for i, j in up]
        last = lax.slice_in_dim(value, length - width, length, axis=dim)
        leading = lax.slice_in_dim(value, 0, width, axis=dim)
        before = lax.ppermute(last, axis, up)
        after = lax.ppermute(leading, axis, down)
        value = jnp.concatenate([before, value, after], axis=dim)
    return value


def pad_cols(values):
    return jnp.pad(values, ((0, 0), (0, 0), (1, 1), (0, 0)))


def conv_fwd(padded, weight, count):
    width = padded.shape[2] - 2
    total = None
    for row_off in range(3):
        for col_off in range(3):
            window = padded[:, row_off : row_off + count, col_off : col_off + width]
            term = jnp.einsum(
                "frwc,cd->frwd",
                window,
                weight[3 * row_off + col_off],
                preferred_element_type=jnp.float32,
            )
            total = term if total is None else total + term
    return total


def conv_back(padded, weight, count):
    width = padded.shape[2] - 2
    total = None
    for row_off in range(3):
        for col_off in range(3):
            window = padded[:, 2 - row_off : 2 - row_off + count, 2 - col_off : 2 - col_off + width]
            term = jnp.einsum(
                "frwd,cd->frwc",
                window,
                weight[3 * row_off + col_off],
                preferred_element_type=jnp.float32,
            )
            total = term if total is None else total + term
    return total


def weight_grad(padded, upstream):
    count = upstream.shape[1]
    width = upstream.shape[2]
    pieces = []
    for row_off in range(3):
        for col_off in range(3):
            window = padded[:, row_off : row_off + count, col_off : col_off + width]
            pieces.append(
                jnp.einsum("frwc,frwd->cd", window, upstream, preferred_element_type=jnp.float32)
            )
    return jnp.stack(pieces)


def silu_slope(pre):
    sig = jax.nn.sigmoid(pre)
    return sig * (1.0 + pre * (1.0 - sig))


def temporal_backward(mixed, upstream, attn_weight):
    frames, pixels, width = mixed.shape
    head_size = width // HEADS
    f32 = jnp.float32
    bf16 = jnp.bfloat16
    mixed_f = mixed.astype(f32)
    norm_scale = lax.rsqrt(jnp.mean(mixed_f * mixed_f, axis=-1, keepdims=True) + EPSILON)
    normed = (mixed_f * norm_scale).astype(bf16).reshape(frames * pixels, width)
    joined = jnp.concatenate([attn_weight[0], attn_weight[1], attn_weight[2]], axis=1)
    projected = jnp.dot(normed, joined, preferred_element_type=f32).astype(bf16)
    shaped = projected.reshape(frames, pixels, 3, HEADS, head_size)
    queries = shaped[:, :, 0]
    keys_all = shaped[:, :, 1]
    values_all = shaped[:, :, 2]
    factor = head_size ** (-0.5)
    scores = jnp.einsum("fqhd,gqhd->qhfg", queries, keys_all, preferred_element_type=f32) * factor
    expo = jnp.exp(scores)
    probs = expo / jnp.sum(expo, axis=-1, keepdims=True)
    probs_low = probs.astype(bf16)
    attended = (
        jnp.einsum("qhfg,gqhd->fqhd", probs_low, values_all, preferred_element_type=f32)
        .astype(bf16)
        .reshape(frames * pixels, width)
    )
    upstream_flat = upstream.reshape(frames * pixels, width)
    grad_att = lax.dot_general(
        upstream_flat, attn_weight[3], (((1,), (1,)), ((), ())), preferred_element_type=f32
    ).astype(bf16)
    out_grad = lax.dot_general(
        attended, upstream_flat, (((0,), (0,)), ((), ())), preferred_element_type=f32
    )
    grad_heads = grad_att.reshape(frames, pixels, HEADS, head_size)
    grad_probs = jnp.einsum("fqhd,gqhd->qhfg", grad_heads, values_all, preferred_element_type=f32)
    grad_values = jnp.einsum(
        "qhfg,fqhd->gqhd", probs_low, grad_heads, preferred_element_type=f32
    ).astype(bf16)
    grad_scores = probs * (grad_probs - jnp.sum(probs * grad_probs, axis=-1, keepdims=True))
    scores_low = (grad_scores * factor).astype(bf16)
    grad_queries = jnp.einsum(
        "qhfg,gqhd->fqhd", scores_low, keys_all, preferred_element_type=f32
    ).astype(bf16)
    grad_keys = jnp.einsum(
        "qhfg,fqhd->gqhd", scores_low, queries, preferred_element_type=f32
    ).astype(bf16)
    grad_joined = jnp.concatenate(
        [
            grad_queries.reshape(frames * pixels, width),
            grad_keys.reshape(frames * pixels, width),
            grad_values.reshape(frames * pixels, width),
        ],
        axis=1,
    )
    grad_normed = lax.dot_general(
        grad_joined, joined, (((1,), (1,)), ((), ())), preferred_element_type=f32
    ).reshape(frames, pixels, width)
    proj_grad = lax.dot_general(
        normed, grad_joined, (((0,), (0,)), ((), ())), preferred_element_type=f32
    )
    inner = jnp.mean(grad_normed * mixed_f, axis=-1, keepdims=True)
    grad_mixed = norm_scale * grad_normed - mixed_f * norm_scale * norm_scale * norm_scale * inner
    total_grad = (upstream.astype(f32) + grad_mixed).astype(bf16)
    weights_grad = jnp.stack(
        [proj_grad[:, :width], proj_grad[:, width : 2 * width], proj_grad[:, 2 * width :], out_grad]
    )
    return (total_grad, weights_grad)


def per_device(frames_in, grad_out, conv_weight, attn_weight):
    frame_count, row_count, width, chans = frames_in.shape
    f32 = jnp.float32
    bf16 = jnp.bfloat16
    inputs_f = frames_in.astype(f32)
    band_count = lax.axis_size("rows")
    in_pad = pad_cols(extended(frames_in, (("rows", 1),), 1))
    hidden_pre = conv_fwd(in_pad, conv_weight[0], row_count)
    hidden_act = jax.nn.silu(hidden_pre).astype(bf16)
    act_pad = pad_cols(extended(hidden_act, (("rows", 1),), 1))
    branch = conv_fwd(act_pad, conv_weight[1], row_count)
    mixed = (inputs_f + branch).astype(bf16)
    flat_mixed = mixed.reshape(frame_count, row_count * width, chans)
    flat_grad = grad_out.reshape(frame_count, row_count * width, chans)
    pixel_mixed, pixel_grad = (
        lax.all_to_all(flat_mixed, "tm", split_axis=1, concat_axis=0, tiled=True),
        lax.all_to_all(flat_grad, "tm", split_axis=1, concat_axis=0, tiled=True),
    )
    pixel_total, attn_sums = temporal_backward(pixel_mixed, pixel_grad, attn_weight)
    returned = lax.all_to_all(pixel_total, "tm", split_axis=0, concat_axis=1, tiled=True)
    grad_mixed = returned.reshape(frame_count, row_count, width, chans)
    second = weight_grad(act_pad, grad_mixed)
    grad_pad = pad_cols(extended(grad_mixed, (("rows", 1),), 1))
    act_grad = conv_back(grad_pad, conv_weight[1], row_count).astype(bf16)
    pre_grad = (act_grad.astype(f32) * silu_slope(hidden_pre)).astype(bf16)
    pre_pad = pad_cols(extended(pre_grad, (("rows", 1),), 1))
    first = weight_grad(in_pad, pre_grad)
    input_grad = (grad_mixed.astype(f32) + conv_back(pre_pad, conv_weight[0], row_count)).astype(
        bf16
    )
    conv_sums = jnp.stack([first, second])
    conv_sums, attn_sums = (
        lax.psum(conv_sums.astype(jnp.bfloat16), "rows").astype(jnp.float32),
        lax.psum(attn_sums.astype(jnp.bfloat16), "rows").astype(jnp.float32),
    )
    conv_sums, attn_sums = (
        lax.psum_scatter(
            conv_sums.astype(jnp.bfloat16), "tm", scatter_dimension=2, tiled=True
        ).astype(jnp.float32),
        lax.psum_scatter(
            attn_sums.astype(jnp.bfloat16), "tm", scatter_dimension=1, tiled=True
        ).astype(jnp.float32),
    )
    positions = frame_count * lax.axis_size("tm") * row_count * band_count * width
    scale = float(positions) ** (-0.5)
    return (input_grad, conv_sums * scale, attn_sums * scale)


def solution(mesh):
    return jax.shard_map(
        per_device,
        mesh=mesh,
        in_specs=(P("tm", "rows", None, None), P("tm", "rows", None, None), P(), P()),
        out_specs=(P("tm", "rows", None, None), P(None, None, "tm", None), P(None, "tm", None)),
        check_vma=False,
    )
```

profile of v0, /device:TPU:4, one launch (start us, length us, event | category | flops | bytes accessed | tf_op | source)
XLA Modules:
  0.0 449.5 jit_solution(216209440748736936)
XLA Ops:
  8.1 3.1 collective-permute-start
  14.4 3.3 collective-permute-done.1
  31.6 5.8 %collective-permute-start.2 = (bf16[1,1,160,256]{3,2,1,0:T(8,128)(2,1)}, bf16[1,1,160,256]{3,2,1,0:T(8,128)(2,1)S(1)}, u32[]{:S(2)}, u32[]{:S(2)}) collective-permute-start(bf16[1,1,160,256]{3,2,1,0:T(8,128)(2,1)} %get-tuple-element.15), channel_id=1, source_target_pairs={{0,1},{1,2},{2,3},{3,4},{4,5},{5,6},{6,7},{8,9},{9,10},{10,11},{11... | collective-permute-start | bytes 245768 | tf_op jit(solution)/shard_map/ppermute | solution.py:19
  40.7 3.6 reduce.4
  45.2 10.9 %all-to-all-start = ((bf16[32,2,3840]{2,1,0:T(2,128)(2,1)}), bf16[32,2,3840]{2,1,0:T(2,128)(2,1)}, u32[]{:S(2)}, u32[]{:S(2)}) async-start(bf16[32,2,3840]{2,1,0:T(2,128)(2,1)} %reshape.464), calls=%async_computation | async-start | bytes 983040 | tf_op jit(solution)/shard_map/all_to_all | solution.py:162
  68.0 4.4 reduce.5
  74.4 10.3 %all-to-all-start.1 = ((bf16[32,2,3840]{2,1,0:T(2,128)(2,1)}), bf16[32,2,3840]{2,1,0:T(2,128)(2,1)}, u32[]{:S(2)}, u32[]{:S(2)}) async-start(bf16[32,2,3840]{2,1,0:T(2,128)(2,1)} %reshape.466), calls=%async_computation.1 | async-start | bytes 983040 | tf_op jit(solution)/shard_map/all_to_all | solution.py:161
  92.3 3.8 convert_reduce_fusion
  101.4 3.4 reshape.467
  109.7 5.7 %reshape.394 = bf16[32,30,3,4,64]{4,3,2,1,0:T(4,128)(2,1)} reshape(bf16[960,768]{1,0:T(8,128)(2,1)} %convolution_convert_fusion) | data formatting | bytes 2949120 | tf_op jit(solution)/shard_map/reshape | solution.py:89
  123.7 5.8 %fusion.21 = bf16[32,30,4,64]{3,0,2,1:T(8,128)(2,1)} fusion(f32[30,4,32,32]{2,3,1,0:T(8,128)} %fusion.101, bf16[32,30,1,4,64]{4,3,2,1,0:T(4,128)(2,1)} %copy-done.3, f32[30,4,32,32]{2,3,1,0:T(8,128)} %copy-done.6, f32[30,4,32]{2,1,0:T(4,128)} %copy-done.19), kind=kOutput, calls=%fused_computation.21 | convolution fusion | flops 17084192 | bytes 1981440 | tf_op jit(solution)/shard_map/qhfg,fqhd->gqhd/dot_general | solution.py:120
  129.5 5.9 %fusion.24 = bf16[32,30,4,64]{3,0,2,1:T(8,128)(2,1)} fusion(f32[30,4,32,32]{2,3,1,0:T(8,128)} %fusion.101, bf16[32,30,1,4,64]{4,3,2,1,0:T(4,128)(2,1)} %copy-done.2, f32[30,4,32,32]{2,3,1,0:T(8,128)} %copy-done.6, f32[30,4,32]{2,1,0:T(4,128)} %copy-done.19), kind=kOutput, calls=%fused_computation.22 | convolution fusion | flops 17084192 | bytes 1981440 | tf_op jit(solution)/shard_map/qhfg,gqhd->fqhd/dot_general | solution.py:117
  160.2 3.1 add_convert_fusion
  163.2 7.0 %all-to-all-start.2 = ((bf16[32,30,256]{2,1,0:T(8,128)(2,1)}), bf16[32,30,256]{2,1,0:T(8,128)(2,1)}, u32[]{:S(2)}, u32[]{:S(2)}) async-start(bf16[32,30,256]{2,1,0:T(8,128)(2,1)} %add_convert_fusion), calls=%async_computation.2 | async-start | bytes 1048576 | tf_op jit(solution)/shard_map/all_to_all | solution.py:165
  182.2 5.3 %all-to-all-done.2 = bf16[32,30,256]{2,1,0:T(8,128)(2,1)} async-done(((bf16[32,30,256]{2,1,0:T(8,128)(2,1)}), bf16[32,30,256]{2,1,0:T(8,128)(2,1)}, u32[]{:S(2)}, u32[]{:S(2)}) %all-to-all-start.2) | async-done | bytes 491552 | tf_op jit(solution)/shard_map/all_to_all | solution.py:165
  191.8 3.4 collective-permute-start.5
  211.1 3.6 copy.99
  214.7 5.7 %reshape.459 = bf16[256,4608]{1,0:T(8,128)(2,1)} reshape(bf16[256,2,9,256]{3,2,1,0:T(8,128)(2,1)} %bitcast.576) | data formatting | bytes 4718592
  220.4 51.9 %reduce-scatter.9.cloned.1.call-done = bf16[8,1024]{1,0:T(8,128)(2,1)} async-done(((bf16[256,1024]{1,0:T(8,128)(2,1)}), bf16[8,1024]{1,0:T(8,128)(2,1)}) %reduce-scatter.9.cloned.1.call-update) | async-done | bytes 16400
  273.0 30.3 %psum.17 = bf16[4,8,256]{2,1,0:T(8,128)(2,1)S(1)} all-reduce(bf16[4,8,256]{2,1,0:T(8,128)(2,1)S(1)} %copy.63), channel_id=1, replica_groups=mesh['tm'=32,'rows'=8] {'rows'}, use_global_device_ids=true, to_apply=%region_6.7 | all-reduce | flops 8192 | bytes 32768 | tf_op jit(solution)/shard_map/psum | solution.py:179
  303.3 3.1 collective-permute-start.6
  310.0 5.1 %collective-permute-done.7 = bf16[1,1,160,256]{3,2,1,0:T(8,128)(2,1)S(1)} collective-permute-done((bf16[1,1,160,256]{3,2,1,0:T(8,128)(2,1)S(1)}, bf16[1,1,160,256]{3,2,1,0:T(8,128)(2,1)S(1)}, u32[]{:S(2)}, u32[]{:S(2)}) %collective-permute-start.7) | collective-permute-done | bytes 81952 | tf_op jit(solution)/shard_map/ppermute | solution.py:20
  327.1 39.5 %reduce-scatter.7.cloned.1.call-done = bf16[8,4608]{1,0:T(8,128)(2,1)} async-done(((bf16[256,4608]{1,0:T(8,128)(2,1)}), bf16[8,4608]{1,0:T(8,128)(2,1)}) %reduce-scatter.7.cloned.1.call-update) | async-done | bytes 73744
  370.9 70.3 %all-reduce.6.cloned.1.call-done = bf16[2,9,8,256]{3,2,1,0:T(8,128)(2,1)} async-done(((bf16[2,9,8,256]{3,2,1,0:T(8,128)(2,1)}), bf16[2,9,8,256]{3,2,1,0:T(8,128)(2,1)}) %all-reduce.6.cloned.1.call-update) | async-done | bytes 73744 | tf_op jit(solution)/shard_map/psum | solution.py:178
  (172 shorter events, 140.7 us)
Async XLA Ops:
  8.1 6.3 %collective-permute-start = (bf16[1,1,160,256]{3,2,1,0:T(8,128)(2,1)S(1)}, bf16[1,1,160,256]{3,2,1,0:T(8,128)(2,1)S(1)}, u32[]{:S(2)}, u32[]{:S(2)}) collective-permute-start(bf16[1,1,160,256]{3,2,1,0:T(8,128)(2,1)S(1)} %get-tuple-element.17), channel_id=1, source_target_pairs={{0,1},{1,2},{2,3},{3,4},{4,5},{5,6},{6,7},{8,9},{9,10},{10,11},{11... | collective-permute-start | bytes 245768 | tf_op jit(solution)/shard_map/ppermute | solution.py:19
  11.2 10.1 %copy-start = (bf16[1,6,160,256]{3,2,1,0:T(8,128)(2,1)S(1)}, bf16[1,6,160,256]{3,2,1,0:T(8,128)(2,1)}, u32[]{:S(2)}) copy-start(bf16[1,6,160,256]{3,2,1,0:T(8,128)(2,1)} %param.4) | copy-start | bytes 1474564
  11.2 6.5 %collective-permute-start.1 = (bf16[1,1,160,256]{3,2,1,0:T(8,128)(2,1)S(1)}, bf16[1,1,160,256]{3,2,1,0:T(8,128)(2,1)S(1)}, u32[]{:S(2)}, u32[]{:S(2)}) collective-permute-start(bf16[1,1,160,256]{3,2,1,0:T(8,128)(2,1)S(1)} %get-tuple-element.18), channel_id=1, source_target_pairs={{1,0},{2,1},{3,2},{4,3},{5,4},{6,5},{7,6},{9,8},{10,9},{11,10},{12... | collective-permute-start | bytes 245768 | tf_op jit(solution)/shard_map/ppermute | solution.py:20
  17.7 10.9 %copy-start.17 = (bf16[1,1,160,256]{3,2,1,0:T(8,128)(2,1)}, bf16[1,1,160,256]{3,2,1,0:T(8,128)(2,1)S(1)}, u32[]{:S(2)}) copy-start(bf16[1,1,160,256]{3,2,1,0:T(8,128)(2,1)S(1)} %collective-permute-done.1) | copy-start | bytes 245764
  28.6 10.8 %copy-start.11 = (bf16[1,6,160,256]{3,2,1,0:T(8,128)(2,1)S(1)}, bf16[1,6,160,256]{3,2,1,0:T(8,128)(2,1)}, u32[]{:S(2)}) copy-start(bf16[1,6,160,256]{3,2,1,0:T(8,128)(2,1)} %param.5) | copy-start | bytes 1474564
  31.6 24.5 %collective-permute-start.2 = (bf16[1,1,160,256]{3,2,1,0:T(8,128)(2,1)}, bf16[1,1,160,256]{3,2,1,0:T(8,128)(2,1)S(1)}, u32[]{:S(2)}, u32[]{:S(2)}) collective-permute-start(bf16[1,1,160,256]{3,2,1,0:T(8,128)(2,1)} %get-tuple-element.15), channel_id=1, source_target_pairs={{0,1},{1,2},{2,3},{3,4},{4,5},{5,6},{6,7},{8,9},{9,10},{10,11},{11... | collective-permute-start | bytes 245768 | tf_op jit(solution)/shard_map/ppermute | solution.py:19
  37.4 18.7 %collective-permute-start.3 = (bf16[1,1,160,256]{3,2,1,0:T(8,128)(2,1)S(1)}, bf16[1,1,160,256]{3,2,1,0:T(8,128)(2,1)S(1)}, u32[]{:S(2)}, u32[]{:S(2)}) collective-permute-start(bf16[1,1,160,256]{3,2,1,0:T(8,128)(2,1)S(1)} %get-tuple-element.16), channel_id=1, source_target_pairs={{1,0},{2,1},{3,2},{4,3},{5,4},{6,5},{7,6},{9,8},{10,9},{11,10},{12... | collective-permute-start | bytes 245768 | tf_op jit(solution)/shard_map/ppermute | solution.py:20
  45.2 29.2 %all-to-all-start = ((bf16[32,2,3840]{2,1,0:T(2,128)(2,1)}), bf16[32,2,3840]{2,1,0:T(2,128)(2,1)}, u32[]{:S(2)}, u32[]{:S(2)}) async-start(bf16[32,2,3840]{2,1,0:T(2,128)(2,1)} %reshape.464), calls=%async_computation | async-start | bytes 983040 | tf_op jit(solution)/shard_map/all_to_all | solution.py:162
  56.1 2.6 copy-start.12
  72.4 12.3 %copy-start.10 = (bf16[4,256,256]{2,1,0:T(8,128)(2,1)S(1)}, bf16[4,256,256]{2,1,0:T(8,128)(2,1)}, u32[]{:S(2)}) copy-start(bf16[4,256,256]{2,1,0:T(8,128)(2,1)} %param.7) | copy-start | bytes 1572868
  74.4 26.9 %all-to-all-start.1 = ((bf16[32,2,3840]{2,1,0:T(2,128)(2,1)}), bf16[32,2,3840]{2,1,0:T(2,128)(2,1)}, u32[]{:S(2)}, u32[]{:S(2)}) async-start(bf16[32,2,3840]{2,1,0:T(2,128)(2,1)} %reshape.466), calls=%async_computation.1 | async-start | bytes 983040 | tf_op jit(solution)/shard_map/all_to_all | solution.py:161
  119.5 2.6 copy-start.6
  119.5 2.6 copy-start.19
  153.8 2.3 copy-start.14
  153.8 2.3 copy-start.15
  153.8 2.3 copy-start.16
  163.2 24.3 %all-to-all-start.2 = ((bf16[32,30,256]{2,1,0:T(8,128)(2,1)}), bf16[32,30,256]{2,1,0:T(8,128)(2,1)}, u32[]{:S(2)}, u32[]{:S(2)}) async-start(bf16[32,30,256]{2,1,0:T(8,128)(2,1)} %add_convert_fusion), calls=%async_computation.2 | async-start | bytes 1048576 | tf_op jit(solution)/shard_map/all_to_all | solution.py:165
  170.2 102.1 %reduce-scatter.9.cloned.1.call-start = ((), (), s32[]{:S(2)}) async-start(), calls=%async_computation.7 | async-start | bytes 540672
  182.2 184.5 %reduce-scatter.7.cloned.1.call-start = ((), (), s32[]{:S(2)}) async-start(), calls=%async_computation.6 | async-start | bytes 2433024
  189.4 11.1 %collective-permute-start.4 = (bf16[1,1,160,256]{3,2,1,0:T(8,128)(2,1)}, bf16[1,1,160,256]{3,2,1,0:T(8,128)(2,1)}, u32[]{:S(2)}, u32[]{:S(2)}) collective-permute-start(bf16[1,1,160,256]{3,2,1,0:T(8,128)(2,1)} %get-tuple-element.13), channel_id=1, source_target_pairs={{0,1},{1,2},{2,3},{3,4},{4,5},{5,6},{6,7},{8,9},{9,10},{10,11},{11... | collective-permute-start | bytes 245768 | tf_op jit(solution)/shard_map/ppermute | solution.py:19
  191.8 8.7 %collective-permute-start.5 = (bf16[1,1,160,256]{3,2,1,0:T(8,128)(2,1)}, bf16[1,1,160,256]{3,2,1,0:T(8,128)(2,1)}, u32[]{:S(2)}, u32[]{:S(2)}) collective-permute-start(bf16[1,1,160,256]{3,2,1,0:T(8,128)(2,1)} %get-tuple-element.14), channel_id=1, source_target_pairs={{1,0},{2,1},{3,2},{4,3},{5,4},{6,5},{7,6},{9,8},{10,9},{11,10},{12... | collective-permute-start | bytes 245768 | tf_op jit(solution)/shard_map/ppermute | solution.py:20
  220.4 220.8 %all-reduce.6.cloned.1.call-start = ((), (), s32[]{:S(2)}) async-start(), calls=%async_computation.5 | async-start | bytes 147456 | tf_op jit(solution)/shard_map/psum | solution.py:178
  303.3 6.7 %collective-permute-start.6 = (bf16[1,1,160,256]{3,2,1,0:T(8,128)(2,1)S(1)}, bf16[1,1,160,256]{3,2,1,0:T(8,128)(2,1)S(1)}, u32[]{:S(2)}, u32[]{:S(2)}) collective-permute-start(bf16[1,1,160,256]{3,2,1,0:T(8,128)(2,1)S(1)} %get-tuple-element.11), channel_id=1, source_target_pairs={{0,1},{1,2},{2,3},{3,4},{4,5},{5,6},{6,7},{8,9},{9,10},{10,11},{11... | collective-permute-start | bytes 245768 | tf_op jit(solution)/shard_map/ppermute | solution.py:19
  306.4 8.7 %collective-permute-start.7 = (bf16[1,1,160,256]{3,2,1,0:T(8,128)(2,1)S(1)}, bf16[1,1,160,256]{3,2,1,0:T(8,128)(2,1)S(1)}, u32[]{:S(2)}, u32[]{:S(2)}) collective-permute-start(bf16[1,1,160,256]{3,2,1,0:T(8,128)(2,1)S(1)} %get-tuple-element.12), channel_id=1, source_target_pairs={{1,0},{2,1},{3,2},{4,3},{5,4},{6,5},{7,6},{9,8},{10,9},{11,10},{12... | collective-permute-start | bytes 245768 | tf_op jit(solution)/shard_map/ppermute | solution.py:20
  (11 other events, 16.7 us)
Sparse Core Ops, SparseCore 0:
  182.3 89.9 reduce-scatter.8
  276.2 90.4 reduce-scatter.6
  370.0 71.1 all-reduce.5
where the time goes:
time: 458 us; the launch traced here: 450 us
  waiting for transfers between devices  179 us (39%)
  matrix products  77.7 us (17%)
  local copies, waits for them, and re-layouts  72.3 us (16%)
  starting transfers between devices  54.1 us (12%)
  blocking collectives  30.3 us (7%)
  other arithmetic  21.6 us (5%)
  between operations  14.8 us (3%)
    unnamed x5, waiting for transfers between devices  91.4 us
    psum x1, waiting for transfers between devices, per_device(): lax.psum(conv_sums.astype(jnp.bfloat16), 'rows').astype(jnp.float32)  70.3 us
    psum x1, blocking collectives, per_device(): lax.psum(attn_sums.astype(jnp.bfloat16), 'rows').astype(jnp.float32)  30.3 us
    unnamed x57, local copies, waits for them, and re-layouts  26.9 us
    dot_general x18, matrix products, conv_fwd(): jnp.einsum('frwc,cd->frwd', window, weight[3 * row_off + col_off], prefer...  22.7 us
    dot_general x18, matrix products, conv_back(): jnp.einsum('frwd,cd->frwc', window, weight[3 * row_off + col_off], prefer...  19.4 us
    ppermute x4, starting transfers between devices, extended(): before = lax.ppermute(last, axis, up)  14.5 us
    ppermute x4, starting transfers between devices, extended(): after = lax.ppermute(leading, axis, down)  11.1 us
  transfers between devices with their start and end apart: 14, of which 8 were waited for; matrix products, arithmetic and copies ran while one was open for 20% of the time, Pallas kernels for 0%

commit v1 on v0

v1 whole, which is shorter than its diff:
```python
import functools

import jax
import jax.numpy as jnp
from jax import lax
from jax.experimental import pallas as pl
from jax.experimental.pallas import tpu as pltpu
from jax.sharding import PartitionSpec as P

HEADS = 4
EPSILON = 1e-06
T, R = 32, 8
NR, W, C = 6, 160, 256
PIX = 32
CHUNKS = NR * W // PIX
EARLY, LATE = 96, 80
F32, BF16 = jnp.float32, jnp.bfloat16
MESH = pl.DeviceIdType.MESH
VMEM_LIMIT = 60 * 1024 * 1024


def barrier(tm, rows, row_peers):
    sem = pltpu.get_barrier_semaphore()

    def tell_tm(s, _):
        pl.semaphore_signal(
            sem, inc=1, device_id={"tm": lax.rem(tm + s, T)}, device_id_type=MESH
        )
        return 0

    lax.fori_loop(1, T, tell_tm, 0)
    for s in row_peers:
        pl.semaphore_signal(
            sem, inc=1, device_id={"rows": lax.rem(rows + s, R)}, device_id_type=MESH
        )
    pl.semaphore_wait(sem, T - 1 + len(row_peers))


def chunk_copy(src, dst, ss, rs, mine, peer, slot):
    return pltpu.make_async_remote_copy(
        src_ref=src.at[peer],
        dst_ref=dst.at[slot],
        send_sem=ss.at[peer],
        recv_sem=rs.at[slot],
        device_id={"tm": peer},
        device_id_type=MESH,
    )


def spread_start(src, dst, ss, rs, tm):
    def go(s, _):
        peer = lax.rem(tm + s, T)
        chunk_copy(src, dst, ss, rs, tm, peer, tm).start()
        return 0

    lax.fori_loop(1, T, go, 0)
    dst[tm] = src[tm]


def spread_wait(src, dst, ss, rs, tm):
    def go(s, _):
        peer = lax.rem(tm + T - s, T)
        copy = chunk_copy(src, dst, ss, rs, tm, peer, peer)
        copy.wait_send()
        copy.wait_recv()
        return 0

    lax.fori_loop(1, T, go, 0)


def row_copy(src, dst, ss, rs, peer):
    return pltpu.make_async_remote_copy(
        src_ref=src,
        dst_ref=dst,
        send_sem=ss,
        recv_sem=rs,
        device_id={"rows": peer},
        device_id_type=MESH,
    )


def shifts(row):
    col = lax.broadcasted_iota(jnp.int32, (W, C), 0)
    before = jnp.where(col == 0, 0.0, pltpu.roll(row, 1, 0))
    after = jnp.where(col == W - 1, 0.0, pltpu.roll(row, W - 1, 0))
    return before, row, after


def fill(src, dst, first, count, forward):
    def go(i, _):
        before, here, after = shifts(src[i].astype(F32))
        parts = (before, here, after) if forward else (after, here, before)
        for b in range(3):
            dst[i, :, b * C : (b + 1) * C] = parts[b].astype(BF16)
        return 0

    lax.fori_loop(first, first + count, go, 0)


def taps(wide, start, count, forward):
    pieces = []
    for a in range(3):
        off = a if forward else 2 - a
        pieces.append(wide[pl.ds(start + off, count)].reshape(count * W, 3 * C))
    return jnp.concatenate(pieces, axis=1)


def forward_kernel(
    x_ref, g_ref, w_ref,
    xe, ae, slope, mt, gt, kt,
    gpad, mpad, xc, ac, hid,
    gs, gr, ms, mr, hs, hr,
):
    tm, rows = lax.axis_index("tm"), lax.axis_index("rows")
    up, down = lax.rem(rows + R - 1, R), lax.rem(rows + 1, R)
    gpad[0:CHUNKS] = g_ref[...]
    gpad[CHUNKS:T] = jnp.zeros((T - CHUNKS, PIX, C), BF16)
    mpad[CHUNKS:T] = jnp.zeros((T - CHUNKS, PIX, C), BF16)
    barrier(tm, rows, (1, R - 1))
    to_up = row_copy(x_ref.at[pl.ds(0, 2)], xe.at[pl.ds(NR + 2, 2)], hs.at[0], hr.at[0], up)
    to_down = row_copy(x_ref.at[pl.ds(NR - 2, 2)], xe.at[pl.ds(0, 2)], hs.at[1], hr.at[1], down)
    to_up.start()
    to_down.start()
    spread_start(gpad, gt, gs, gr, tm)
    xe[2 : NR + 2] = x_ref[...]
    fill(xe, xc, 2, NR, True)
    to_up.wait()
    to_down.wait()

    @pl.when(rows == 0)
    def _():
        xe[0:2] = jnp.zeros((2, W, C), BF16)

    @pl.when(rows == R - 1)
    def _():
        xe[NR + 2 : NR + 4] = jnp.zeros((2, W, C), BF16)

    fill(xe, xc, 0, 2, True)
    fill(xe, xc, NR + 2, 2, True)

    def first(i, _):
        s = i * 2
        hidden = jnp.dot(taps(xc, s, 2, True), w_ref[0], preferred_element_type=F32)
        hidden = hidden.reshape(2, W, C)
        hid[pl.ds(s, 2)] = hidden
        ae[pl.ds(s, 2)] = (hidden * jax.nn.sigmoid(hidden)).astype(BF16)
        return 0

    lax.fori_loop(0, 4, first, 0)

    @pl.when(rows == 0)
    def _():
        ae[0:1] = jnp.zeros((1, W, C), BF16)

    @pl.when(rows == R - 1)
    def _():
        ae[NR + 1 : NR + 2] = jnp.zeros((1, W, C), BF16)

    fill(ae, ac, 0, NR + 2, True)

    def second(i, _):
        s = i * 2
        branch = jnp.dot(taps(ac, s, 2, True), w_ref[1], preferred_element_type=F32)
        mixed = x_ref[pl.ds(s, 2)].astype(F32).reshape(2 * W, C) + branch
        mpad[pl.ds(i * 10, 10)] = mixed.astype(BF16).reshape(10, PIX, C)
        return 0

    lax.fori_loop(0, 3, second, 0)
    spread_start(mpad, mt, ms, mr, tm)

    def turn(i, _):
        for k in range(2):
            at = pl.ds(pl.multiple_of(i * C, C), C)
            kt[k, at, :] = w_ref[k, at, :].astype(F32).T.astype(BF16)
        return 0

    lax.fori_loop(0, 9, turn, 0)

    def slopes(i, _):
        h = hid[i]
        s = jax.nn.sigmoid(h)
        slope[i] = s * (1.0 + h * (1.0 - s))
        return 0

    lax.fori_loop(0, NR + 2, slopes, 0)
    spread_wait(gpad, gt, gs, gr, tm)
    spread_wait(mpad, mt, ms, mr, tm)


def nt(a, b):
    return lax.dot_general(a, b, (((1,), (1,)), ((), ())), preferred_element_type=F32)


def tn(a, b):
    return lax.dot_general(a, b, (((0,), (0,)), ((), ())), preferred_element_type=F32)


def attention_kernel(mt, gt, aw, out, wg, stage, stage_g, mix, gup, normed, scale, qkv, ga, att, gj):
    joined = jnp.concatenate([aw[0], aw[1], aw[2]], axis=1)
    n = T * PIX

    def widen(f, _):
        at = pl.ds(pl.multiple_of(f * PIX, PIX), PIX)
        for half in range(2):
            cols = pl.ds(half * 128, 128)
            stage[half, at, :] = mt[f, :, cols].astype(F32)
            stage_g[half, at, :] = gt[f, :, cols].astype(F32)
        return 0

    lax.fori_loop(0, T, widen, 0)

    def by_pixel(p, _):
        at = pl.ds(pl.multiple_of(p * T, T), T)
        m = jnp.concatenate([stage[h, pl.ds(p, T, stride=PIX), :] for h in range(2)], axis=1)
        g = jnp.concatenate([stage_g[h, pl.ds(p, T, stride=PIX), :] for h in range(2)], axis=1)
        ns = lax.rsqrt(jnp.mean(m * m, axis=-1, keepdims=True) + EPSILON)
        mix[at, :] = m
        scale[at, :] = jnp.broadcast_to(ns, (T, 128))
        normed[at, :] = (m * ns).astype(BF16)
        gup[at, :] = g.astype(BF16)
        return 0

    lax.fori_loop(0, PIX, by_pixel, 0)
    step = 256
    for i in range(n // step):
        at = slice(i * step, (i + 1) * step)
        qkv[at, :] = jnp.dot(normed[at, :], joined, preferred_element_type=F32).astype(BF16)
        ga[at, :] = nt(gup[at, :], aw[3]).astype(BF16)

    factor = 64.0**-0.5
    g = 128
    lane = lax.broadcasted_iota(jnp.int32, (1, C), 1) // 64
    head = [(lane == h).astype(F32).astype(BF16) for h in range(HEADS)]
    blocks = (
        lax.rem(lax.broadcasted_iota(jnp.int32, (HEADS * g, g), 0), g) // T
        == lax.broadcasted_iota(jnp.int32, (HEADS * g, g), 1) // T
    )

    def stack(x):
        return jnp.concatenate([x * head[h] for h in range(HEADS)], axis=0)

    def side(x):
        return jnp.concatenate([x[h * g : (h + 1) * g] for h in range(HEADS)], axis=1)

    def group(i, _):
        at = pl.ds(pl.multiple_of(i * g, g), g)
        q, k, v = qkv[at, 0:C], qkv[at, C : 2 * C], qkv[at, 2 * C : 3 * C]
        a = ga[at, :]
        qs, ks, vs, gas = stack(q), stack(k), stack(v), stack(a)
        expo = jnp.where(blocks, jnp.exp(nt(qs, k) * factor), 0.0)
        probs = expo / jnp.sum(expo, axis=-1, keepdims=True)
        low = probs.astype(BF16)
        att[at, :] = jnp.dot(side(low), vs, preferred_element_type=F32).astype(BF16)
        gp = nt(gas, v)
        gs = probs * (gp - jnp.sum(probs * gp, axis=-1, keepdims=True))
        sl = (gs * factor).astype(BF16)
        gj[at, 0:C] = jnp.dot(side(sl), ks, preferred_element_type=F32).astype(BF16)
        gj[at, C : 2 * C] = tn(sl, qs).astype(BF16)
        gj[at, 2 * C : 3 * C] = tn(low, gas).astype(BF16)
        return 0

    lax.fori_loop(0, n // g, group, 0)
    for i in range(n // step):
        at = slice(i * step, (i + 1) * step)
        gn = nt(gj[at, :], joined)
        m = mix[at, :]
        ns = jnp.concatenate([scale[at, :]] * 2, axis=1)
        inner = jnp.mean(gn * m, axis=-1, keepdims=True)
        total = gup[at, :].astype(F32) + (ns * gn - m * ns * ns * ns * inner)
        for h in range(2):
            stage[h, at, :] = total[:, h * 128 : (h + 1) * 128]

    def by_frame(f, _):
        for h in range(2):
            out[f, :, pl.ds(h * 128, 128)] = stage[h, pl.ds(f, PIX, stride=T), :].astype(BF16)
        return 0

    lax.fori_loop(0, T, by_frame, 0)
    proj = tn(normed[...], gj[...])
    for k in range(3):
        wg[k] = proj[:, k * C : (k + 1) * C]
    wg[3] = tn(att[...], gup[...])


def slab(t):
    z, y, c = t // 8, (t // 2) % 4, t % 2
    return c, y * 4 + z


def pack(dst, row, upper, lower):
    for t in range(T):
        c, k = slab(t)
        both = jnp.concatenate([upper[t * 8 : t * 8 + 8], lower[t * 8 : t * 8 + 8]], axis=0)
        dst[c, k, row : row + 16, :] = both.astype(BF16)


class Reduction:
    def __init__(self, n, packed, r1, a1, r2, a2, r3, a3, r4, ss, rs, tm, rows):
        self.n, self.packed, self.r1, self.a1, self.r2 = n, packed, r1, a1, r2
        self.a2, self.r3, self.a3, self.r4 = a2, r3, a3, r4
        self.ss, self.rs, self.tm, self.rows = ss, rs, tm, rows
        self.core, self.y, self.z = lax.rem(tm, 2), lax.rem(tm // 2, 4), tm // 8

    def copy(self, src, dst, s, dev):
        return pltpu.make_async_remote_copy(
            src_ref=src, dst_ref=dst, send_sem=self.ss.at[s], recv_sem=self.rs.at[s],
            device_id=dev, device_id_type=MESH,
        )

    def core_copy(self):
        return self.copy(
            self.packed.at[1 - self.core], self.r1, 0, {"tm": self.tm + 1 - 2 * self.core}
        )

    def y_copy(self, s):
        y = lax.rem(self.y + s, 4)
        return self.copy(
            self.a1.at[y], self.r2.at[s - 1], s, {"tm": self.z * 8 + y * 2 + self.core}
        )

    def z_copy(self, s):
        z = lax.rem(self.z + s, 4)
        return self.copy(
            self.a2.at[z], self.r3.at[s - 1], 3 + s, {"tm": z * 8 + self.y * 2 + self.core}
        )

    def row_copy(self, s):
        peer = lax.rem(self.rows + s, R)
        return self.copy(self.a3, self.r4.at[s - 1], 6 + s, {"rows": peer})

    def start(self):
        self.core_copy().start()

    def after_core(self):
        self.core_copy().wait()

        def add(k, _):
            y, z = k // 4, lax.rem(k, 4)
            self.a1[y, z] = (
                self.packed[self.core, k].astype(F32) + self.r1[k].astype(F32)
            ).astype(BF16)
            return 0

        lax.fori_loop(0, 16, add, 0)
        for s in (1, 2, 3):
            self.y_copy(s).start()

    def after_y(self):
        for s in (1, 2, 3):
            self.y_copy(s).wait()

        def add(z, _):
            total = self.a1[self.y, z].astype(F32)
            for s in range(3):
                total += self.r2[s, z].astype(F32)
            self.a2[z] = total.astype(BF16)
            return 0

        lax.fori_loop(0, 4, add, 0)
        for s in (1, 2, 3):
            self.z_copy(s).start()

    def after_z(self):
        for s in (1, 2, 3):
            self.z_copy(s).wait()
        total = self.a2[self.z].astype(F32)
        for s in range(3):
            total += self.r3[s].astype(F32)
        self.a3[...] = total.astype(BF16)
        for s in range(1, R):
            self.row_copy(s).start()

    def finish(self):
        for s in range(1, R):
            self.row_copy(s).wait()
        self.r4[R - 1] = self.a3[...]
        total = jnp.zeros((self.n, C), F32)
        for row in range(R):
            slot = lax.rem(self.rows + 2 * R - row - 1, R)
            total += self.r4[slot].astype(F32)
        return total * (float(T * NR * R * W) ** -0.5)


def backward_kernel(
    pt, wg, xe, ae, slope, kt,
    dx, dconv, dattn,
    gm, ge, uc, pre, pc, g1,
    ps, pr, hs, hr,
    *bufs,
):
    tm, rows = lax.axis_index("tm"), lax.axis_index("rows")
    up, down = lax.rem(rows + R - 1, R), lax.rem(rows + 1, R)
    early = Reduction(EARLY, *bufs[:10], tm, rows)
    late = Reduction(LATE, *bufs[10:], tm, rows)
    barrier(tm, rows, tuple(range(1, R)))
    spread_start(pt, gm, ps, pr, tm)
    pack(early.packed, 64, wg[0], wg[1])
    pack(early.packed, 80, wg[2], wg[3])
    spread_wait(pt, gm, ps, pr, tm)
    ge[2 : NR + 2] = gm[0:CHUNKS].reshape(NR, W, C)
    to_up = row_copy(ge.at[pl.ds(2, 2)], ge.at[pl.ds(NR + 2, 2)], hs.at[0], hr.at[0], up)
    to_down = row_copy(ge.at[pl.ds(NR, 2)], ge.at[pl.ds(0, 2)], hs.at[1], hr.at[1], down)
    to_up.start()
    to_down.start()
    fill(ge, uc, 2, NR, False)
    for a in range(3):
        g1[a] = tn(
            ae[a : a + NR].reshape(NR * W, C), uc[2 : NR + 2].reshape(NR * W, 3 * C)
        )

    def one(k):
        return g1[k // 3, :, (k % 3) * C : (k % 3 + 1) * C]

    for k in range(0, 8, 2):
        pack(early.packed, k * 8, one(k), one(k + 1))
    early.start()
    to_up.wait()
    to_down.wait()

    @pl.when(rows == 0)
    def _():
        ge[0:2] = jnp.zeros((2, W, C), BF16)

    @pl.when(rows == R - 1)
    def _():
        ge[NR + 2 : NR + 4] = jnp.zeros((2, W, C), BF16)

    fill(ge, uc, 0, 2, False)
    fill(ge, uc, NR + 2, 2, False)

    def first(i, _):
        s = i * 2
        act_grad = jnp.dot(taps(uc, s, 2, False), kt[1], preferred_element_type=F32)
        act_grad = act_grad.astype(BF16).astype(F32).reshape(2, W, C)
        pre[pl.ds(s, 2)] = (act_grad * slope[pl.ds(s, 2)]).astype(BF16)
        return 0

    lax.fori_loop(0, 4, first, 0)

    @pl.when(rows == 0)
    def _():
        pre[0:1] = jnp.zeros((1, W, C), BF16)

    @pl.when(rows == R - 1)
    def _():
        pre[NR + 1 : NR + 2] = jnp.zeros((1, W, C), BF16)

    early.after_core()
    fill(pre, pc, 0, NR + 2, False)
    last = g1[2, :, 2 * C : 3 * C]
    g0 = []
    for a in range(3):
        g0.append(
            tn(xe[a + 1 : a + 1 + NR].reshape(NR * W, C), pc[1 : NR + 1].reshape(NR * W, 3 * C))
        )

    def zero(k):
        return g0[k // 3][:, (k % 3) * C : (k % 3 + 1) * C]

    for k in range(0, 8, 2):
        pack(late.packed, k * 8, zero(k), zero(k + 1))
    pack(late.packed, 64, zero(8), last)
    late.start()

    def second(i, _):
        s = i * 2
        back = jnp.dot(taps(pc, s, 2, False), kt[0], preferred_element_type=F32)
        here = ge[pl.ds(s + 2, 2)].astype(F32).reshape(2 * W, C)
        dx[pl.ds(s, 2)] = (here + back).astype(BF16).reshape(2, W, C)
        return 0

    lax.fori_loop(0, 3, second, 0)
    early.after_y()
    late.after_core()
    early.after_z()
    late.after_y()
    sums = early.finish()
    dconv[1, 0:8] = sums[0:64].reshape(8, 8, C)
    dattn[...] = sums[64:96].reshape(4, 8, C)
    late.after_z()
    sums = late.finish()
    dconv[0] = sums[0:72].reshape(9, 8, C)
    dconv[1, 8:9] = sums[72:80].reshape(1, 8, C)


def vmem(count):
    return [pl.BlockSpec(memory_space=pltpu.VMEM)] * count


def dma(count):
    return pltpu.SemaphoreType.DMA((count,))


def params(collective_id):
    if collective_id is None:
        return pltpu.CompilerParams(vmem_limit_bytes=VMEM_LIMIT)
    return pltpu.CompilerParams(
        vmem_limit_bytes=VMEM_LIMIT, collective_id=collective_id, has_side_effects=True
    )


def sum_buffers(n):
    return [
        pltpu.VMEM((2, 16, n, C), BF16),
        pltpu.VMEM((16, n, C), BF16),
        pltpu.VMEM((4, 4, n, C), BF16),
        pltpu.VMEM((3, 4, n, C), BF16),
        pltpu.VMEM((4, n, C), BF16),
        pltpu.VMEM((3, n, C), BF16),
        pltpu.VMEM((n, C), BF16),
        pltpu.VMEM((R, n, C), BF16),
        dma(14),
        dma(14),
    ]


def per_device(frames_in, grad_out, conv_weight, attn_weight):
    x = frames_in.reshape(NR, W, C)
    g = grad_out.reshape(CHUNKS, PIX, C)
    w = conv_weight.reshape(2, 9 * C, C)
    spread = jax.ShapeDtypeStruct((T, PIX, C), BF16)
    xe, ae, slope, mt, gt, kt = pl.pallas_call(
        forward_kernel,
        out_shape=[
            jax.ShapeDtypeStruct((NR + 4, W, C), BF16),
            jax.ShapeDtypeStruct((NR + 2, W, C), BF16),
            jax.ShapeDtypeStruct((NR + 2, W, C), F32),
            spread,
            spread,
            jax.ShapeDtypeStruct((2, 9 * C, C), BF16),
        ],
        in_specs=vmem(3),
        out_specs=vmem(6),
        scratch_shapes=[
            pltpu.VMEM((T, PIX, C), BF16),
            pltpu.VMEM((T, PIX, C), BF16),
            pltpu.VMEM((NR + 4, W, 3 * C), BF16),
            pltpu.VMEM((NR + 2, W, 3 * C), BF16),
            pltpu.VMEM((NR + 2, W, C), F32),
            dma(T), dma(T), dma(T), dma(T), dma(2), dma(2),
        ],
        compiler_params=params(1),
        name="forward",
    )(x, g, w)
    n = T * PIX
    pt, wg = pl.pallas_call(
        attention_kernel,
        out_shape=[spread, jax.ShapeDtypeStruct((4, C, C), F32)],
        in_specs=vmem(3),
        out_specs=vmem(2),
        scratch_shapes=[
            pltpu.VMEM((2, n, 128), F32),
            pltpu.VMEM((2, n, 128), F32),
            pltpu.VMEM((n, C), F32),
            pltpu.VMEM((n, C), BF16),
            pltpu.VMEM((n, C), BF16),
            pltpu.VMEM((n, 128), F32),
            pltpu.VMEM((n, 3 * C), BF16),
            pltpu.VMEM((n, C), BF16),
            pltpu.VMEM((n, C), BF16),
            pltpu.VMEM((n, 3 * C), BF16),
        ],
        compiler_params=params(None),
        name="attention",
    )(mt, gt, attn_weight)
    dx, dconv, dattn = pl.pallas_call(
        backward_kernel,
        out_shape=[
            jax.ShapeDtypeStruct((NR, W, C), BF16),
            jax.ShapeDtypeStruct((2, 9, 8, C), F32),
            jax.ShapeDtypeStruct((4, 8, C), F32),
        ],
        in_specs=vmem(6),
        out_specs=vmem(3),
        scratch_shapes=[
            pltpu.VMEM((T, PIX, C), BF16),
            pltpu.VMEM((NR + 4, W, C), BF16),
            pltpu.VMEM((NR + 4, W, 3 * C), BF16),
            pltpu.VMEM((NR + 2, W, C), BF16),
            pltpu.VMEM((NR + 2, W, 3 * C), BF16),
            pltpu.VMEM((3, C, 3 * C), F32),
            dma(T), dma(T), dma(2), dma(2),
            *sum_buffers(EARLY),
            *sum_buffers(LATE),
        ],
        compiler_params=params(2),
        name="backward",
    )(pt, wg, xe, ae, slope, kt)
    return dx.reshape(1, NR, W, C), dconv, dattn


def solution(mesh):
    return jax.shard_map(
        per_device,
        mesh=mesh,
        in_specs=(P("tm", "rows", None, None), P("tm", "rows", None, None), P(), P()),
        out_specs=(P("tm", "rows", None, None), P(None, None, "tm", None), P(None, "tm", None)),
        check_vma=False,
    )
```

time: 458 us -> 135 us (0.29); the launches traced: 450 us -> 134 us
  waiting for transfers between devices: 179 us -> 0 us
  Pallas kernels: 0 us -> 129 us
  matrix products: 77.7 us -> 0 us
  local copies, waits for them, and re-layouts: 72.3 us -> 4.79 us
  starting transfers between devices: 54.1 us -> 0 us
  blocking collectives: 30.3 us -> 0 us
  other arithmetic: 21.6 us -> 0 us
  between operations: 14.8 us -> 0.65 us
    pallas_call x0 -> x3, Pallas kernels: none -> 129 us  [the longest x1 71 us: per_device(): pl.pallas_call(backward_kernel, out_shape=[jax.ShapeDtypeStruct((NR, W, C...]
    unnamed x5 -> x0, waiting for transfers between devices: 91.4 us -> none
    dot_general x65 -> x0, matrix products: 77.7 us -> none  [the longest x18 22.7 us: conv_fwd(): jnp.einsum('frwc,cd->frwd', window, weight[3 * row_off + col_off], prefer...]
    psum x1 -> x0, waiting for transfers between devices: 70.3 us -> none  [per_device(): lax.psum(conv_sums.astype(jnp.bfloat16), 'rows').astype(jnp.float32)]
    psum x1 -> x0, blocking collectives: 30.3 us -> none  [per_device(): lax.psum(attn_sums.astype(jnp.bfloat16), 'rows').astype(jnp.float32)]
    all_to_all x3 -> x0, starting transfers between devices: 28.1 us -> none  [the longest x1 10.9 us: per_device(): lax.all_to_all(flat_grad, 'tm', split_axis=1, concat_axis=0, tiled=True)]
    ppermute x8 -> x0, starting transfers between devices: 25.6 us -> none  [the longest x4 14.5 us: extended(): before = lax.ppermute(last, axis, up)]
    reshape x11 -> x0, local copies, waits for them, and re-layouts: 25.3 us -> none  [the longest x1 5.7 us: temporal_backward(): shaped = projected.reshape(frames, pixels, 3, HEADS, head_size)]
  transfers between devices with their start and end apart: 14 -> 0, of which waited for: 8 -> 0; matrix products, arithmetic and copies ran while one was open for 20% -> 0% of each run, Pallas kernels for 0% -> 0%
where the time goes in v1:
time: 135 us; the launch traced here: 134 us
  Pallas kernels  129 us (96%)
  local copies, waits for them, and re-layouts  4.79 us (4%)
    pallas_call x1, Pallas kernels, per_device(): pl.pallas_call(backward_kernel, out_shape=[jax.ShapeDtypeStruct((NR, W, C...  71 us
    pallas_call x1, Pallas kernels, per_device(): pl.pallas_call(forward_kernel, out_shape=[jax.ShapeDtypeStruct((NR + 4, W...  39.4 us
    pallas_call x1, Pallas kernels, per_device(): pl.pallas_call(attention_kernel, out_shape=[spread, jax.ShapeDtypeStruct(...  18.5 us
    unnamed x3, local copies, waits for them, and re-layouts  4.79 us

profile of v1, /device:TPU:4, one launch (start us, length us, event | category | flops | bytes accessed | tf_op | source)
XLA Modules:
  0.0 134.3 jit_solution(12446451757540787487)
XLA Ops:
  0.6 39.4 %forward.1 = (bf16[10,160,256]{2,1,0:T(8,128)(2,1)}, bf16[8,160,256]{2,1,0:T(8,128)(2,1)}, f32[8,160,256]{2,1,0:T(8,128)}, bf16[32,32,256]{2,1,0:T(8,128)(2,1)},...) custom-call(bf16[6,160,256]{2,1,0:T(8,128)(2,1)} %bitcast.5, bf16[30,32,256]{2,1,0:T(8,128)(2,1)} %bitcast.6, ...), custom_call_target="tpu_custom_call" | custom-call | tf_op jit(solution)/shard_map/forward/pallas_call | solution.py:522
  40.1 18.5 %attention.1 = (bf16[32,32,256]{2,1,0:T(8,128)(2,1)}, f32[4,256,256]{2,1,0:T(8,128)}) custom-call(bf16[32,32,256]{2,1,0:T(8,128)(2,1)} %get-tuple-element.14.mt, bf16[32,32,256]{2,1,0:T(8,128)(2,1)} %get-tuple-element.15.gt, bf16[4,256,256]{2,1,0:T(8,128)(2,1)} %aw.1), custom_call_target="tpu_custom_call" | custom-call | tf_op jit(solution)/shard_map/attention/pallas_call | solution.py:546
  58.6 71.0 %backward.1 = (bf16[6,160,256]{2,1,0:T(8,128)(2,1)}, f32[2,9,8,256]{3,2,1,0:T(8,128)}, f32[4,8,256]{2,1,0:T(8,128)}) custom-call(bf16[32,32,256]{2,1,0:T(8,128)(2,1)} %get-tuple-element.16.pt, f32[4,256,256]{2,1,0:T(8,128)} %get-tuple-element.17.wg, bf16[10,160,256]{2,1,0:T(8,128)(2,1)} %get-tuple-element.18.xe, bf16[8,160,256]{2,1,0:T(8,128)(2,1)} %get-tuple-element.19.ae, ...), custom_call_target="tpu_custom_call" | custom-call | tf_op jit(solution)/shard_map/backward/pallas_call | solution.py:566
  129.5 1.8 %copy.10 = bf16[1,6,160,256]{3,2,1,0:T(8,128)(2,1)} copy(bf16[1,6,160,256]{3,2,1,0:T(8,128)(2,1)} %bitcast.7) | data formatting | bytes 983040
  131.4 1.6 %copy.11 = f32[2,9,8,256]{3,2,1,0:T(8,128)} copy(f32[2,9,8,256]{3,2,1,0:T(8,128)} %get-tuple-element.29) | data formatting | bytes 294912
  133.0 1.4 %copy.12 = f32[4,8,256]{2,1,0:T(8,128)} copy(f32[4,8,256]{2,1,0:T(8,128)} %get-tuple-element.30) | data formatting | bytes 65536

commit v2 on v0

v2 whole, which is shorter than its diff:
```python
import functools

import jax
import jax.numpy as jnp
from jax import lax
from jax.experimental import pallas as pl
from jax.experimental.pallas import tpu as pltpu
from jax.sharding import PartitionSpec as P

HEADS = 4
EPSILON = 1e-06
T, R = 32, 8
NR, W, C = 6, 160, 256
PIX = 16
UNROLL = 2
EARLY, LATE = 96, 80
F32, BF16 = jnp.float32, jnp.bfloat16
MESH = pl.DeviceIdType.MESH
VMEM_LIMIT = 60 * 1024 * 1024


def signal(sem, device):
    pl.semaphore_signal(sem, inc=1, device_id=device, device_id_type=MESH)


def barrier(tm, rows):
    sem = pltpu.get_barrier_semaphore()

    def tell_tm(s, _):
        signal(sem, {"tm": lax.rem(tm + s, T)})
        return 0

    lax.fori_loop(1, T, tell_tm, 0)
    for s in range(1, R):
        signal(sem, {"rows": lax.rem(rows + s, R)})
    for s in (8, 16, 24):
        signal(sem, {"tm": lax.rem(tm + s, T), "rows": lax.rem(rows + 4, R)})
    pl.semaphore_wait(sem, T - 1 + R - 1 + 3)


def remote(src, dst, ss, rs, device):
    return pltpu.make_async_remote_copy(
        src_ref=src,
        dst_ref=dst,
        send_sem=ss,
        recv_sem=rs,
        device_id=device,
        device_id_type=MESH,
    )


def chunk_copy(bufs, half, peer, slot):
    src, dst, ss, rs = bufs
    return remote(
        src.at[half, peer], dst.at[half, slot], ss.at[half, peer], rs.at[half, slot], {"tm": peer}
    )


def spread_start(bufs, half, tm):
    def go(s, _):
        chunk_copy(bufs, half, lax.rem(tm + s, T), tm).start()
        return 0

    lax.fori_loop(1, T, go, 0)
    bufs[1][half, tm] = bufs[0][half, tm]


def spread_wait(bufs, half, tm):
    def go(s, _):
        peer = lax.rem(tm + T - s, T)
        copy = chunk_copy(bufs, half, peer, peer)
        copy.wait_send()
        copy.wait_recv()
        return 0

    lax.fori_loop(1, T, go, 0)


def shifts(row):
    col = lax.broadcasted_iota(jnp.int32, (W, C), 0)
    before = jnp.where(col == 0, 0.0, pltpu.roll(row, 1, 0))
    after = jnp.where(col == W - 1, 0.0, pltpu.roll(row, W - 1, 0))
    return before, row, after


def fill(src, dst, first, count, forward):
    def go(i, _):
        before, here, after = shifts(src[i].astype(F32))
        parts = (before, here, after) if forward else (after, here, before)
        for b in range(3):
            dst[i, :, b * C : (b + 1) * C] = parts[b].astype(BF16)
        return 0

    lax.fori_loop(first, first + count, go, 0)


def taps(wide, start, count, forward):
    pieces = []
    for a in range(3):
        off = a if forward else 2 - a
        pieces.append(wide[start + off : start + off + count].reshape(count * W, 3 * C))
    return jnp.concatenate(pieces, axis=1)


def conv(wide, runs, weight, forward):
    lhs = [taps(wide, start, count, forward) for start, count in runs]
    lhs = lhs[0] if len(lhs) == 1 else jnp.concatenate(lhs, axis=0)
    out = jnp.dot(lhs, weight, preferred_element_type=F32)
    return out.reshape(out.shape[0] // W, W, C)


def nt(a, b):
    return lax.dot_general(a, b, (((1,), (1,)), ((), ())), preferred_element_type=F32)


def tn(a, b):
    return lax.dot_general(a, b, (((0,), (0,)), ((), ())), preferred_element_type=F32)


def attend(half, mt, gt, pt, aw, joined, work, unroll):
    stage, stage_g, mix, scale, qkv, ga, gup, normed, att, gj = work
    n = T * PIX
    base = half * n

    def widen(f, _):
        at = pl.ds(pl.multiple_of(f * PIX, PIX), PIX)
        for h in range(2):
            cols = pl.ds(h * 128, 128)
            stage[h, at, :] = mt[half, f, :, cols].astype(F32)
            stage_g[h, at, :] = gt[half, f, :, cols].astype(F32)
        return 0

    lax.fori_loop(0, T, widen, 0, unroll=4)

    def by_pixel(p, _):
        at = pl.ds(pl.multiple_of(p * T, T), T)
        to = pl.ds(pl.multiple_of(base + p * T, T), T)
        m = jnp.concatenate([stage[h, pl.ds(p, T, stride=PIX), :] for h in range(2)], axis=1)
        g = jnp.concatenate([stage_g[h, pl.ds(p, T, stride=PIX), :] for h in range(2)], axis=1)
        ns = lax.rsqrt(jnp.mean(m * m, axis=-1, keepdims=True) + EPSILON)
        mix[at, :] = m
        scale[at, :] = jnp.broadcast_to(ns, (T, 128))
        normed[to, :] = (m * ns).astype(BF16)
        gup[to, :] = g.astype(BF16)
        return 0

    lax.fori_loop(0, PIX, by_pixel, 0, unroll=4)
    every = pl.ds(base, n)
    qkv[...] = jnp.dot(normed[every, :], joined[...], preferred_element_type=F32).astype(BF16)
    ga[...] = nt(gup[every, :], aw[3]).astype(BF16)

    factor = 64.0**-0.5
    g = 128
    lane = lax.broadcasted_iota(jnp.int32, (1, C), 1) // 64
    head = [(lane == h).astype(F32).astype(BF16) for h in range(HEADS)]
    blocks = (
        lax.rem(lax.broadcasted_iota(jnp.int32, (HEADS * g, g), 0), g) // T
        == lax.broadcasted_iota(jnp.int32, (HEADS * g, g), 1) // T
    )

    def stack(x):
        return jnp.concatenate([x * head[h] for h in range(HEADS)], axis=0)

    def side(x):
        return jnp.concatenate([x[h * g : (h + 1) * g] for h in range(HEADS)], axis=1)

    def group(i, _):
        at = pl.ds(pl.multiple_of(i * g, g), g)
        to = pl.ds(pl.multiple_of(base + i * g, g), g)
        q, k, v = qkv[at, 0:C], qkv[at, C : 2 * C], qkv[at, 2 * C : 3 * C]
        qs, ks, vs, gas = stack(q), stack(k), stack(v), stack(ga[at, :])
        expo = jnp.where(blocks, jnp.exp(nt(qs, k) * factor), 0.0)
        probs = expo / jnp.sum(expo, axis=-1, keepdims=True)
        low = probs.astype(BF16)
        att[to, :] = jnp.dot(side(low), vs, preferred_element_type=F32).astype(BF16)
        gp = nt(gas, v)
        gs = probs * (gp - jnp.sum(probs * gp, axis=-1, keepdims=True))
        sl = (gs * factor).astype(BF16)
        gj[to, 0:C] = jnp.dot(side(sl), ks, preferred_element_type=F32).astype(BF16)
        gj[to, C : 2 * C] = tn(sl, qs).astype(BF16)
        gj[to, 2 * C : 3 * C] = tn(low, gas).astype(BF16)
        return 0

    lax.fori_loop(0, n // g, group, 0, unroll=unroll)
    step = 256
    for i in range(n // step):
        at = slice(i * step, (i + 1) * step)
        to = slice(base + i * step, base + (i + 1) * step)
        gn = nt(gj[to, :], joined[...])
        m = mix[at, :]
        ns = jnp.concatenate([scale[at, :]] * 2, axis=1)
        inner = jnp.mean(gn * m, axis=-1, keepdims=True)
        total = gup[to, :].astype(F32) + (ns * gn - m * ns * ns * ns * inner)
        for h in range(2):
            stage[h, at, :] = total[:, h * 128 : (h + 1) * 128]

    def by_frame(f, _):
        for h in range(2):
            pt[half, f, :, pl.ds(h * 128, 128)] = stage[h, pl.ds(f, PIX, stride=T), :].astype(BF16)
        return 0

    lax.fori_loop(0, T, by_frame, 0, unroll=4)


def attend_buffers():
    n = T * PIX
    return [
        pltpu.VMEM((2, n, 128), F32),
        pltpu.VMEM((2, n, 128), F32),
        pltpu.VMEM((n, C), F32),
        pltpu.VMEM((n, 128), F32),
        pltpu.VMEM((n, 3 * C), BF16),
        pltpu.VMEM((n, C), BF16),
        pltpu.VMEM((2 * n, C), BF16),
        pltpu.VMEM((2 * n, C), BF16),
        pltpu.VMEM((2 * n, C), BF16),
        pltpu.VMEM((2 * n, 3 * C), BF16),
    ]


class Reduction:
    count = 13

    @staticmethod
    def buffers(n, nx):
        ny = n - nx
        shapes = [
            (2, 4, 4, nx), (2, 4, 4, ny),
            (4, 4, nx), (4, 4, ny),
            (4, 4, nx), (4, 4, ny),
            (3, 4, nx), (3, 4, ny),
            (3, nx), (3, ny),
            (n,),
            (8, n),
            (n,),
        ]
        return [pltpu.VMEM(s + (C,), BF16) for s in shapes] + [dma(30), dma(30)]

    def __init__(self, n, nx, bufs, tm, rows):
        self.n, self.nx, self.cut = n, nx, 48
        self.px, self.py, self.rx1, self.ry1, self.ax1, self.ay1 = bufs[0:6]
        self.rx2, self.ry2, self.rx3, self.ry3, self.a3, self.r4, self.out = bufs[6:13]
        self.ss, self.rs = bufs[13:15]
        self.core, self.y, self.z_hi = lax.rem(tm, 2), lax.rem(tm // 2, 4), tm // 8
        self.x, self.z_lo = lax.rem(rows, 4), rows // 4
        self.tm, self.rows = tm, rows

    def copy(self, src, dst, s, r, device):
        return remote(src, dst, self.ss.at[s], self.rs.at[r], device)

    def pack(self, row, upper, lower):
        for t in range(T):
            z, y, c = t // 8, (t // 2) % 4, t % 2
            both = jnp.concatenate([upper[t * 8 : t * 8 + 8], lower[t * 8 : t * 8 + 8]], axis=0)
            if row < self.nx:
                self.px[c, z, y, row : row + 16, :] = both.astype(BF16)
            else:
                self.py[c, y, z, row - self.nx : row - self.nx + 16, :] = both.astype(BF16)

    def tm_at(self, z_hi, y):
        return {"tm": z_hi * 8 + y * 2 + self.core}

    def row_at(self, z_lo, x):
        return {"rows": z_lo * 4 + x}

    def first(self):
        other = {"tm": self.tm + 1 - 2 * self.core}
        return (
            self.copy(self.px.at[1 - self.core], self.rx1, 0, 0, other),
            self.copy(self.py.at[1 - self.core], self.ry1, 1, 1, other),
        )

    def second(self):
        copies = []
        for s in (1, 2, 3):
            x, y = lax.rem(self.x + s, 4), lax.rem(self.y + s, 4)
            copies.append(
                self.copy(
                    self.ax1.at[x], self.rx2.at[s - 1], 1 + s, 1 + s, self.row_at(self.z_lo, x)
                )
            )
            copies.append(
                self.copy(
                    self.ay1.at[y], self.ry2.at[s - 1], 4 + s, 4 + s, self.tm_at(self.z_hi, y)
                )
            )
        return copies

    def third(self):
        copies = []
        for s in (1, 2, 3):
            x, y = lax.rem(self.x + s, 4), lax.rem(self.y + s, 4)
            copies.append(
                self.copy(
                    self.ax1.at[self.x, y],
                    self.rx3.at[s - 1], 7 + s, 7 + s, self.tm_at(self.z_hi, y),
                )
            )
            copies.append(
                self.copy(
                    self.ay1.at[self.y, x],
                    self.ry3.at[s - 1], 10 + s, 10 + s, self.row_at(self.z_lo, x),
                )
            )
        return copies

    def piece(self, k):
        return pl.ds(0, self.cut) if k == 0 else pl.ds(self.cut, self.n - self.cut)

    def fourth(self, k):
        z = self.z_hi * 2 + self.z_lo
        at = self.piece(k)
        device = {"tm": self.x * 8 + self.y * 2 + self.core, "rows": k * 4 + self.x}
        return self.copy(self.a3.at[at], self.r4.at[z, at], 14 + k, 14 + z, device)

    def fourth_in(self, k, z):
        at = self.piece(k)
        device = {"tm": self.tm, "rows": self.rows}
        return self.copy(self.a3.at[at], self.r4.at[z, at], 14 + k, 14 + z, device)

    def fifth(self, k, s):
        at = self.piece(k)
        peer = lax.rem(self.rows + s, R)
        return self.copy(self.out.at[at], self.out.at[at], 21 + s, 22 + k, {"rows": peer})

    def holds(self, k):
        return jnp.logical_and(self.z_hi == self.x, self.z_lo == k)

    def away(self, k):
        return jnp.logical_not(self.holds(k))

    def start(self):
        for copy in self.first():
            copy.start()

    def after_core(self):
        for copy in self.first():
            copy.wait()

        def add(k, _):
            i, j = k // 4, lax.rem(k, 4)
            for p, r, a in ((self.px, self.rx1, self.ax1), (self.py, self.ry1, self.ay1)):
                a[i, j] = (p[self.core, i, j].astype(F32) + r[i, j].astype(F32)).astype(BF16)
            return 0

        lax.fori_loop(0, 16, add, 0)
        for copy in self.second():
            copy.start()

    def after_second(self):
        for copy in self.second():
            copy.wait()

        def add(j, _):
            for a, r, me in ((self.ax1, self.rx2, self.x), (self.ay1, self.ry2, self.y)):
                total = a[me, j].astype(F32)
                for s in range(3):
                    total += r[s, j].astype(F32)
                a[me, j] = total.astype(BF16)
            return 0

        lax.fori_loop(0, 4, add, 0)
        for copy in self.third():
            copy.start()

    def after_third(self):
        for copy in self.third():
            copy.wait()
        for a, r, i, j, at in (
            (self.ax1, self.rx3, self.x, self.y, pl.ds(0, self.nx)),
            (self.ay1, self.ry3, self.y, self.x, pl.ds(self.nx, self.n - self.nx)),
        ):
            total = a[i, j].astype(F32)
            for s in range(3):
                total += r[s].astype(F32)
            self.a3[at, :] = total.astype(BF16)
        for k in range(2):

            @pl.when(self.away(k))
            def _():
                self.fourth(k).start()

    def after_fourth(self):
        for k in range(2):

            @pl.when(self.away(k))
            def _():
                self.fourth(k).wait_send()

            @pl.when(self.holds(k))
            def _():
                at = self.piece(k)
                mine = self.z_hi * 2 + k

                def arrived(s, _):
                    self.fourth_in(k, lax.rem(mine + s, 8)).wait_recv()
                    return 0

                lax.fori_loop(1, 8, arrived, 0)
                self.r4[mine, at, :] = self.a3[at, :]
                total = self.r4[0, at, :].astype(F32)
                for z in range(1, 8):
                    total += self.r4[z, at, :].astype(F32)
                self.out[at, :] = total.astype(BF16)
                for s in range(1, R):
                    self.fifth(k, s).start()

    def finish(self):
        for k in range(2):

            @pl.when(self.holds(k))
            def _():
                for s in range(1, R):
                    self.fifth(k, s).wait_send()

            @pl.when(self.away(k))
            def _():
                self.fifth(k, 1).wait_recv()

        return self.out[...].astype(F32) * (float(T * NR * R * W) ** -0.5)


def zero_at(ref, where, condition):
    @pl.when(condition)
    def _():
        ref[where] = jnp.zeros(ref[where].shape, ref.dtype)


def block_kernel(
    x_ref, g_ref, w_ref, aw,
    dx, dconv, dattn,
    xe, ae, hid, kt, joined, gpad, gt, mpad, mt, pt, gm,
    xc, ac, ge, uc, pre, pc, g1,
    gs, gr, ms, mr, ps, pr, hs, hr, ks, kr,
    *bufs,
):
    tm, rows = lax.axis_index("tm"), lax.axis_index("rows")
    up = {"rows": lax.rem(rows + R - 1, R)}
    down = {"rows": lax.rem(rows + 1, R)}
    top, bottom = rows == 0, rows == R - 1
    work, bufs = bufs[:10], bufs[10:]
    early = Reduction(EARLY, 48, bufs[:15], tm, rows)
    late = Reduction(LATE, 48, bufs[15:], tm, rows)
    g_bufs, m_bufs, p_bufs = (gpad, gt, gs, gr), (mpad, mt, ms, mr), (pt, gm, ps, pr)

    gpad[0, 0:10] = g_ref[0:1].reshape(10, PIX, C)
    gpad[0, 10:30] = g_ref[4:6].reshape(20, PIX, C)
    gpad[1, 0:30] = g_ref[1:4].reshape(30, PIX, C)
    for half in range(2):
        gpad[half, 30:32] = jnp.zeros((2, PIX, C), BF16)
        mpad[half, 30:32] = jnp.zeros((2, PIX, C), BF16)
    barrier(tm, rows)
    to_up = remote(x_ref.at[pl.ds(0, 2)], xe.at[pl.ds(NR + 2, 2)], hs.at[0], hr.at[0], up)
    to_down = remote(x_ref.at[pl.ds(NR - 2, 2)], xe.at[pl.ds(0, 2)], hs.at[1], hr.at[1], down)
    to_up.start()
    to_down.start()
    spread_start(g_bufs, 0, tm)
    xe[2 : NR + 2] = x_ref[...]
    fill(xe, xc, 2, NR, True)

    def keep(first, hidden):
        hid[first : first + hidden.shape[0]] = hidden
        ae[first : first + hidden.shape[0]] = (hidden * jax.nn.sigmoid(hidden)).astype(BF16)

    keep(2, conv(xc, ((2, 4),), w_ref[0], True))
    spread_start(g_bufs, 1, tm)
    to_up.wait()
    to_down.wait()
    zero_at(xe, slice(0, 2), top)
    zero_at(xe, slice(NR + 2, NR + 4), bottom)
    fill(xe, xc, 0, 2, True)
    fill(xe, xc, NR + 2, 2, True)
    ends = conv(xc, ((0, 2), (6, 2)), w_ref[0], True)
    keep(0, ends[0:2])
    keep(6, ends[2:4])
    zero_at(ae, slice(0, 1), top)
    zero_at(ae, slice(NR + 1, NR + 2), bottom)
    fill(ae, ac, 0, NR + 2, True)
    branch = conv(ac, ((0, 1), (4, 2)), w_ref[1], True)
    mixed = jnp.concatenate([x_ref[0:1], x_ref[4:6]], axis=0).astype(F32) + branch
    mpad[0, 0:30] = mixed.astype(BF16).reshape(30, PIX, C)
    spread_start(m_bufs, 0, tm)
    mixed = x_ref[1:4].astype(F32) + conv(ac, ((1, 3),), w_ref[1], True)
    mpad[1, 0:30] = mixed.astype(BF16).reshape(30, PIX, C)
    spread_start(m_bufs, 1, tm)
    joined[...] = jnp.concatenate([aw[0], aw[1], aw[2]], axis=1)

    def turn(i, _):
        for k in range(2):
            at = pl.ds(pl.multiple_of(i * C, C), C)
            kt[k, at, :] = w_ref[k, at, :].astype(F32).T.astype(BF16)
        return 0

    lax.fori_loop(0, 9, turn, 0)

    def slopes(i, _):
        h = hid[i]
        s = jax.nn.sigmoid(h)
        hid[i] = s * (1.0 + h * (1.0 - s))
        return 0

    lax.fori_loop(0, NR + 2, slopes, 0)
    for half in range(2):
        spread_wait(g_bufs, half, tm)
        spread_wait(m_bufs, half, tm)
        attend(half, mt, gt, pt, aw, joined, work, UNROLL)
        spread_start(p_bufs, half, tm)

    gup, normed, att, gj = work[6:10]
    proj = tn(normed[...], gj[...])
    early.pack(64, proj[:, 0:C], proj[:, C : 2 * C])
    early.pack(80, proj[:, 2 * C : 3 * C], tn(att[...], gup[...]))

    spread_wait(p_bufs, 0, tm)
    ge[2:3] = gm[0, 0:10].reshape(1, W, C)
    ge[6:8] = gm[0, 10:30].reshape(2, W, C)
    near_up = remote(ge.at[2], ge.at[NR + 2], ks.at[0], kr.at[0], up)
    near_down = remote(ge.at[NR + 1], ge.at[1], ks.at[1], kr.at[1], down)
    near_up.start()
    near_down.start()
    fill(ge, uc, 2, 1, False)
    fill(ge, uc, 6, 2, False)

    def stacked(ref, runs):
        return jnp.concatenate([ref[s : s + n].reshape(n * W, ref.shape[2]) for s, n in runs], axis=0)

    for a in range(3):
        g1[a] = tn(stacked(ae, ((a, 1), (a + 4, 2))), stacked(uc, ((2, 1), (6, 2))))
    spread_wait(p_bufs, 1, tm)
    ge[3:6] = gm[1, 0:30].reshape(3, W, C)
    far_up = remote(ge.at[3], ge.at[NR + 3], ks.at[2], kr.at[2], up)
    far_down = remote(ge.at[NR], ge.at[0], ks.at[3], kr.at[3], down)
    far_up.start()
    far_down.start()
    fill(ge, uc, 3, 3, False)
    for a in range(3):
        g1[a] += tn(stacked(ae, ((a + 1, 3),)), stacked(uc, ((3, 3),)))

    def one(k):
        return g1[k // 3, :, (k % 3) * C : (k % 3 + 1) * C]

    for k in range(0, 8, 2):
        early.pack(k * 8, one(k), one(k + 1))
    early.start()

    def back(first, act_grad):
        at = slice(first, first + act_grad.shape[0])
        pre[at] = (act_grad.astype(BF16).astype(F32) * hid[at]).astype(BF16)

    near_up.wait()
    near_down.wait()
    zero_at(ge, slice(1, 2), top)
    zero_at(ge, slice(NR + 2, NR + 3), bottom)
    fill(ge, uc, 1, 1, False)
    fill(ge, uc, NR + 2, 1, False)
    back(1, conv(uc, ((1, 6),), kt[1], False))
    early.after_core()
    fill(pre, pc, 1, NR, False)
    g0 = [
        tn(xe[a + 1 : a + 1 + NR].reshape(NR * W, C), pc[1 : NR + 1].reshape(NR * W, 3 * C))
        for a in range(3)
    ]

    def zero(k):
        return g0[k // 3][:, (k % 3) * C : (k % 3 + 1) * C]

    for k in range(0, 8, 2):
        late.pack(k * 8, zero(k), zero(k + 1))
    late.pack(64, zero(8), one(8))
    late.start()
    early.after_second()
    far_up.wait()
    far_down.wait()
    zero_at(ge, slice(0, 1), top)
    zero_at(ge, slice(NR + 3, NR + 4), bottom)
    fill(ge, uc, 0, 1, False)
    fill(ge, uc, NR + 3, 1, False)
    ends = conv(uc, ((0, 1), (7, 1)), kt[1], False)
    back(0, ends[0:1])
    back(7, ends[1:2])
    zero_at(pre, slice(0, 1), top)
    zero_at(pre, slice(NR + 1, NR + 2), bottom)
    late.after_core()
    early.after_third()
    fill(pre, pc, 0, 1, False)
    fill(pre, pc, NR + 1, 1, False)
    dx[0:3] = (ge[2:5].astype(F32) + conv(pc, ((0, 3),), kt[0], False)).astype(BF16)
    late.after_second()
    dx[3:6] = (ge[5:8].astype(F32) + conv(pc, ((3, 3),), kt[0], False)).astype(BF16)
    early.after_fourth()
    late.after_third()
    sums = early.finish()
    dconv[1, 0:8] = sums[0:64].reshape(8, 8, C)
    dattn[...] = sums[64:96].reshape(4, 8, C)
    late.after_fourth()
    sums = late.finish()
    dconv[0] = sums[0:72].reshape(9, 8, C)
    dconv[1, 8:9] = sums[72:80].reshape(1, 8, C)


def pass_kernel(a, b, c, x, y, z):
    x[...] = a[...]
    y[...] = b[...]
    z[...] = c[...]


def vmem(count):
    return [pl.BlockSpec(memory_space=pltpu.VMEM)] * count


def dma(*shape):
    return pltpu.SemaphoreType.DMA(shape)


def params(collective_id=None):
    if collective_id is None:
        return pltpu.CompilerParams(vmem_limit_bytes=VMEM_LIMIT)
    return pltpu.CompilerParams(
        vmem_limit_bytes=VMEM_LIMIT, collective_id=collective_id, has_side_effects=True
    )


def per_device(frames_in, grad_out, conv_weight, attn_weight):
    x = frames_in.reshape(NR, W, C)
    g = grad_out.reshape(NR, W, C)
    w = conv_weight.reshape(2, 9 * C, C)
    spread = pltpu.VMEM((2, T, PIX, C), BF16)
    shapes = [
        jax.ShapeDtypeStruct((NR, W, C), BF16),
        jax.ShapeDtypeStruct((2, 9, 8, C), F32),
        jax.ShapeDtypeStruct((4, 8, C), F32),
    ]
    outs = pl.pallas_call(
        block_kernel,
        out_shape=shapes,
        in_specs=vmem(4),
        out_specs=vmem(3),
        scratch_shapes=[
            pltpu.VMEM((NR + 4, W, C), BF16),
            pltpu.VMEM((NR + 2, W, C), BF16),
            pltpu.VMEM((NR + 2, W, C), F32),
            pltpu.VMEM((2, 9 * C, C), BF16),
            pltpu.VMEM((C, 3 * C), BF16),
            *[spread] * 6,
            pltpu.VMEM((NR + 4, W, 3 * C), BF16),
            pltpu.VMEM((NR + 2, W, 3 * C), BF16),
            pltpu.VMEM((NR + 4, W, C), BF16),
            pltpu.VMEM((NR + 4, W, 3 * C), BF16),
            pltpu.VMEM((NR + 2, W, C), BF16),
            pltpu.VMEM((NR + 2, W, 3 * C), BF16),
            pltpu.VMEM((3, C, 3 * C), F32),
            *[dma(2, T)] * 6,
            dma(2), dma(2), dma(4), dma(4),
            *attend_buffers(),
            *Reduction.buffers(EARLY, 48),
            *Reduction.buffers(LATE, 48),
        ],
        compiler_params=params(1),
        name="block",
    )(x, g, w, attn_weight)
    dx, dconv, dattn = pl.pallas_call(
        pass_kernel,
        out_shape=shapes,
        in_specs=vmem(3),
        out_specs=vmem(3),
        compiler_params=params(),
        name="hand_on",
    )(*outs)
    return dx.reshape(1, NR, W, C), dconv, dattn


def solution(mesh):
    return jax.shard_map(
        per_device,
        mesh=mesh,
        in_specs=(P("tm", "rows", None, None), P("tm", "rows", None, None), P(), P()),
        out_specs=(P("tm", "rows", None, None), P(None, None, "tm", None), P(None, "tm", None)),
        check_vma=False,
    )
```

time: 458 us -> 103 us (0.22); the launches traced: 450 us -> 102 us
  waiting for transfers between devices: 179 us -> 0 us
  Pallas kernels: 0 us -> 102 us
  matrix products: 77.7 us -> 0 us
  local copies, waits for them, and re-layouts: 72.3 us -> 0 us
  starting transfers between devices: 54.1 us -> 0 us
  blocking collectives: 30.3 us -> 0 us
  other arithmetic: 21.6 us -> 0 us
  between operations: 14.8 us -> 0.64 us
    pallas_call x0 -> x2, Pallas kernels: none -> 102 us  [the longest x1 99.8 us: per_device(): pl.pallas_call(block_kernel, out_shape=shapes, in_specs=vmem(4), out_spec...]
    unnamed x5 -> x0, waiting for transfers between devices: 91.4 us -> none
    dot_general x65 -> x0, matrix products: 77.7 us -> none  [the longest x18 22.7 us: conv_fwd(): jnp.einsum('frwc,cd->frwd', window, weight[3 * row_off + col_off], prefer...]
    psum x1 -> x0, waiting for transfers between devices: 70.3 us -> none  [per_device(): lax.psum(conv_sums.astype(jnp.bfloat16), 'rows').astype(jnp.float32)]
    psum x1 -> x0, blocking collectives: 30.3 us -> none  [per_device(): lax.psum(attn_sums.astype(jnp.bfloat16), 'rows').astype(jnp.float32)]
    all_to_all x3 -> x0, starting transfers between devices: 28.1 us -> none  [the longest x1 10.9 us: per_device(): lax.all_to_all(flat_grad, 'tm', split_axis=1, concat_axis=0, tiled=True)]
    unnamed x57 -> x0, local copies, waits for them, and re-layouts: 26.9 us -> none
    ppermute x8 -> x0, starting transfers between devices: 25.6 us -> none  [the longest x4 14.5 us: extended(): before = lax.ppermute(last, axis, up)]
  transfers between devices with their start and end apart: 14 -> 0, of which waited for: 8 -> 0; matrix products, arithmetic and copies ran while one was open for 20% -> 0% of each run, Pallas kernels for 0% -> 0%
where the time goes in v2:
time: 103 us; the launch traced here: 102 us
  Pallas kernels  102 us (99%)
    pallas_call x1, Pallas kernels, per_device(): pl.pallas_call(block_kernel, out_shape=shapes, in_specs=vmem(4), out_spec...  99.8 us

profile of v2, /device:TPU:4, one launch (start us, length us, event | category | flops | bytes accessed | tf_op | source)
XLA Modules:
  0.0 102.4 jit_solution(5957053446202138077)
XLA Ops:
  0.6 99.8 %block.1 = (bf16[6,160,256]{2,1,0:T(8,128)(2,1)}, f32[2,9,8,256]{3,2,1,0:T(8,128)}, f32[4,8,256]{2,1,0:T(8,128)}) custom-call(bf16[6,160,256]{2,1,0:T(8,128)(2,1)} %bitcast.5, bf16[6,160,256]{2,1,0:T(8,128)(2,1)} %bitcast.6, bf16[2,2304,256]{2,1,0:T(8,128)(2,1)} %bitcast.4, bf16[4,256,256]{2,1,0:T(8,128)(2,1)} %aw.1), custom_call_target="tpu_custom_call" | custom-call | tf_op jit(solution)/shard_map/block/pallas_call | solution.py:633
  100.5 2.0 %hand_on.1 = (bf16[6,160,256]{2,1,0:T(8,128)(2,1)}, f32[2,9,8,256]{3,2,1,0:T(8,128)}, f32[4,8,256]{2,1,0:T(8,128)}) custom-call(bf16[6,160,256]{2,1,0:T(8,128)(2,1)} %get-tuple-element.9.a, f32[2,9,8,256]{3,2,1,0:T(8,128)} %get-tuple-element.10.b, f32[4,8,256]{2,1,0:T(8,128)} %get-tuple-element.11.c), custom_call_target="tpu_custom_call" | custom-call | tf_op jit(solution)/shard_map/hand_on/pallas_call | solution.py:661

commit v3 on v2

--- a/solution.py
+++ b/solution.py
@@ -12,8 +12,7 @@
 T, R = 32, 8
 NR, W, C = 6, 160, 256
 PIX = 16
-UNROLL = 2
-EARLY, LATE = 96, 80
+UNROLL = 4
 F32, BF16 = jnp.float32, jnp.bfloat16
 MESH = pl.DeviceIdType.MESH
 VMEM_LIMIT = 60 * 1024 * 1024
@@ -49,31 +48,29 @@
     )
 
 
-def chunk_copy(bufs, half, peer, slot):
+def spread_start(bufs, half, tm):
     src, dst, ss, rs = bufs
-    return remote(
-        src.at[half, peer], dst.at[half, slot], ss.at[half, peer], rs.at[half, slot], {"tm": peer}
+
+    def go(s, _):
+        peer = lax.rem(tm + s, T)
+        remote(
+            src.at[half, peer], dst.at[half, tm], ss.at[half], rs.at[half], {"tm": peer}
+        ).start()
+        return 0
+
+    lax.fori_loop(1, T, go, 0)
+    dst[half, tm] = src[half, tm]
+
+
+def spread_wait(bufs, half, tm):
+    src, dst, ss, rs = bufs
+    every = pl.ds(0, T - 1)
+    copy = remote(
+        src.at[half, every], dst.at[half, every], ss.at[half], rs.at[half],
+        {"tm": lax.rem(tm + 1, T)},
     )
-
-
-def spread_start(bufs, half, tm):
-    def go(s, _):
-        chunk_copy(bufs, half, lax.rem(tm + s, T), tm).start()
-        return 0
-
-    lax.fori_loop(1, T, go, 0)
-    bufs[1][half, tm] = bufs[0][half, tm]
-
-
-def spread_wait(bufs, half, tm):
-    def go(s, _):
-        peer = lax.rem(tm + T - s, T)
-        copy = chunk_copy(bufs, half, peer, peer)
-        copy.wait_send()
-        copy.wait_recv()
-        return 0
-
-    lax.fori_loop(1, T, go, 0)
+    copy.wait_send()
+    copy.wait_recv()
 
 
 def shifts(row):
@@ -222,11 +219,12 @@
     count = 13
 
     @staticmethod
-    def buffers(n, nx):
+    def buffers(pairs, xp):
+        n, nx = pairs * 16, xp * 16
         ny = n - nx
         shapes = [
-            (2, 4, 4, nx), (2, 4, 4, ny),
-            (4, 4, nx), (4, 4, ny),
+            (pairs, 2, 16, 16),
+            (pairs, 16, 16),
             (4, 4, nx), (4, 4, ny),
             (3, 4, nx), (3, 4, ny),
             (3, nx), (3, ny),
@@ -234,28 +232,23 @@
             (8, n),
             (n,),
         ]
-        return [pltpu.VMEM(s + (C,), BF16) for s in shapes] + [dma(30), dma(30)]
-
-    def __init__(self, n, nx, bufs, tm, rows):
-        self.n, self.nx, self.cut = n, nx, 48
-        self.px, self.py, self.rx1, self.ry1, self.ax1, self.ay1 = bufs[0:6]
-        self.rx2, self.ry2, self.rx3, self.ry3, self.a3, self.r4, self.out = bufs[6:13]
-        self.ss, self.rs = bufs[13:15]
+        return [pltpu.VMEM(s + (C,), BF16) for s in shapes] + [dma(pairs + 7), dma(pairs + 7)]
+
+    def __init__(self, pairs, xp, bufs, tm, rows):
+        self.pairs, self.xp = pairs, xp
+        self.n, self.nx = pairs * 16, xp * 16
+        self.cut = self.nx
+        self.packed, self.r1, self.ax1, self.ay1 = bufs[0:4]
+        self.rx2, self.ry2, self.rx3, self.ry3, self.a3, self.r4, self.out = bufs[4:11]
+        self.ss, self.rs = bufs[11:13]
         self.core, self.y, self.z_hi = lax.rem(tm, 2), lax.rem(tm // 2, 4), tm // 8
         self.x, self.z_lo = lax.rem(rows, 4), rows // 4
         self.tm, self.rows = tm, rows
 
     def copy(self, src, dst, s, r, device):
-        return remote(src, dst, self.ss.at[s], self.rs.at[r], device)
-
-    def pack(self, row, upper, lower):
-        for t in range(T):
-            z, y, c = t // 8, (t // 2) % 4, t % 2
-            both = jnp.concatenate([upper[t * 8 : t * 8 + 8], lower[t * 8 : t * 8 + 8]], axis=0)
-            if row < self.nx:
-                self.px[c, z, y, row : row + 16, :] = both.astype(BF16)
-            else:
-                self.py[c, y, z, row - self.nx : row - self.nx + 16, :] = both.astype(BF16)
+        return remote(
+            src, dst, self.ss.at[self.pairs + s], self.rs.at[self.pairs + r], device
+        )
 
     def tm_at(self, z_hi, y):
         return {"tm": z_hi * 8 + y * 2 + self.core}
@@ -263,46 +256,37 @@
     def row_at(self, z_lo, x):
         return {"rows": z_lo * 4 + x}
 
-    def first(self):
+    def first(self, j):
         other = {"tm": self.tm + 1 - 2 * self.core}
-        return (
-            self.copy(self.px.at[1 - self.core], self.rx1, 0, 0, other),
-            self.copy(self.py.at[1 - self.core], self.ry1, 1, 1, other),
+        return remote(
+            self.packed.at[j, 1 - self.core], self.r1.at[j], self.ss.at[j], self.rs.at[j], other
         )
 
-    def second(self):
-        copies = []
-        for s in (1, 2, 3):
-            x, y = lax.rem(self.x + s, 4), lax.rem(self.y + s, 4)
-            copies.append(
-                self.copy(
-                    self.ax1.at[x], self.rx2.at[s - 1], 1 + s, 1 + s, self.row_at(self.z_lo, x)
-                )
-            )
-            copies.append(
-                self.copy(
-                    self.ay1.at[y], self.ry2.at[s - 1], 4 + s, 4 + s, self.tm_at(self.z_hi, y)
-                )
-            )
-        return copies
-
-    def third(self):
-        copies = []
-        for s in (1, 2, 3):
-            x, y = lax.rem(self.x + s, 4), lax.rem(self.y + s, 4)
-            copies.append(
-                self.copy(
-                    self.ax1.at[self.x, y],
-                    self.rx3.at[s - 1], 7 + s, 7 + s, self.tm_at(self.z_hi, y),
-                )
-            )
-            copies.append(
-                self.copy(
-                    self.ay1.at[self.y, x],
-                    self.ry3.at[s - 1], 10 + s, 10 + s, self.row_at(self.z_lo, x),
-                )
-            )
-        return copies
+    def send(self, j, upper, lower):
+        for t in range(T):
+            both = jnp.concatenate([upper[t * 8 : t * 8 + 8], lower[t * 8 : t * 8 + 8]], axis=0)
+            self.packed[j, t % 2, t // 2] = both.astype(BF16)
+        self.first(j).start()
+
+    def second_x(self, s):
+        x = lax.rem(self.x + s, 4)
+        return self.copy(self.ax1.at[x], self.rx2.at[s - 1], 0, 0, self.row_at(self.z_lo, x))
+
+    def second_y(self, s):
+        y = lax.rem(self.y + s, 4)
+        return self.copy(self.ay1.at[y], self.ry2.at[s - 1], 1, 1, self.tm_at(self.z_hi, y))
+
+    def third_x(self, s):
+        y = lax.rem(self.y + s, 4)
+        return self.copy(
+            self.ax1.at[self.x, y], self.rx3.at[s - 1], 2, 2, self.tm_at(self.z_hi, y)
+        )
+
+    def third_y(self, s):
+        x = lax.rem(self.x + s, 4)
+        return self.copy(
+            self.ay1.at[self.y, x], self.ry3.at[s - 1], 3, 3, self.row_at(self.z_lo, x)
+        )
 
     def piece(self, k):
         return pl.ds(0, self.cut) if k == 0 else pl.ds(self.cut, self.n - self.cut)
@@ -311,17 +295,19 @@
         z = self.z_hi * 2 + self.z_lo
         at = self.piece(k)
         device = {"tm": self.x * 8 + self.y * 2 + self.core, "rows": k * 4 + self.x}
-        return self.copy(self.a3.at[at], self.r4.at[z, at], 14 + k, 14 + z, device)
-
-    def fourth_in(self, k, z):
-        at = self.piece(k)
-        device = {"tm": self.tm, "rows": self.rows}
-        return self.copy(self.a3.at[at], self.r4.at[z, at], 14 + k, 14 + z, device)
+        return self.copy(self.a3.at[at], self.r4.at[z, at], 4 + k, 4, device)
 
     def fifth(self, k, s):
         at = self.piece(k)
         peer = lax.rem(self.rows + s, R)
-        return self.copy(self.out.at[at], self.out.at[at], 21 + s, 22 + k, {"rows": peer})
+        return self.copy(self.out.at[at], self.out.at[at], 6, 5 + k, {"rows": peer})
+
+    def wait(self, src, dst, s, r, send=True, recv=True):
+        copy = self.copy(src, dst, s, r, {"rows": lax.rem(self.rows + 1, R)})
+        if send:
+            copy.wait_send()
+        if recv:
+            copy.wait_recv()
 
     def holds(self, k):
         return jnp.logical_and(self.z_hi == self.x, self.z_lo == k)
@@ -329,47 +315,48 @@
     def away(self, k):
         return jnp.logical_not(self.holds(k))
 
-    def start(self):
-        for copy in self.first():
-            copy.start()
-
     def after_core(self):
-        for copy in self.first():
-            copy.wait()
-
-        def add(k, _):
-            i, j = k // 4, lax.rem(k, 4)
-            for p, r, a in ((self.px, self.rx1, self.ax1), (self.py, self.ry1, self.ay1)):
-                a[i, j] = (p[self.core, i, j].astype(F32) + r[i, j].astype(F32)).astype(BF16)
-            return 0
-
-        lax.fori_loop(0, 16, add, 0)
-        for copy in self.second():
-            copy.start()
+        for j in range(self.pairs):
+            self.first(j).wait()
+            in_x = j < self.xp
+            at = pl.ds((j if in_x else j - self.xp) * 16, 16)
+
+            def add(k, _):
+                z, y = k // 4, lax.rem(k, 4)
+                total = self.packed[j, self.core, k].astype(F32) + self.r1[j, k].astype(F32)
+                if in_x:
+                    self.ax1[z, y, at, :] = total.astype(BF16)
+                else:
+                    self.ay1[y, z, at, :] = total.astype(BF16)
+                return 0
+
+            lax.fori_loop(0, 16, add, 0, unroll=4)
+            if j == self.xp - 1:
+                for s in (1, 2, 3):
+                    self.second_x(s).start()
+        for s in (1, 2, 3):
+            self.second_y(s).start()
 
     def after_second(self):
-        for copy in self.second():
-            copy.wait()
-
-        def add(j, _):
-            for a, r, me in ((self.ax1, self.rx2, self.x), (self.ay1, self.ry2, self.y)):
+        for a, r, me, i, go in (
+            (self.ax1, self.rx2, self.x, 0, self.third_x),
+            (self.ay1, self.ry2, self.y, 1, self.third_y),
+        ):
+            self.wait(r, r, i, i)
+            for j in range(4):
                 total = a[me, j].astype(F32)
                 for s in range(3):
                     total += r[s, j].astype(F32)
                 a[me, j] = total.astype(BF16)
-            return 0
-
-        lax.fori_loop(0, 4, add, 0)
-        for copy in self.third():
-            copy.start()
+            for s in (1, 2, 3):
+                go(s).start()
 
     def after_third(self):
-        for copy in self.third():
-            copy.wait()
-        for a, r, i, j, at in (
-            (self.ax1, self.rx3, self.x, self.y, pl.ds(0, self.nx)),
-            (self.ay1, self.ry3, self.y, self.x, pl.ds(self.nx, self.n - self.nx)),
+        for a, r, i, j, at, sem in (
+            (self.ax1, self.rx3, self.x, self.y, pl.ds(0, self.nx), 2),
+            (self.ay1, self.ry3, self.y, self.x, pl.ds(self.nx, self.n - self.nx), 3),
         ):
+            self.wait(r, r, sem, sem)
             total = a[i, j].astype(F32)
             for s in range(3):
                 total += r[s].astype(F32)
@@ -391,12 +378,8 @@
             def _():
                 at = self.piece(k)
                 mine = self.z_hi * 2 + k
-
-                def arrived(s, _):
-                    self.fourth_in(k, lax.rem(mine + s, 8)).wait_recv()
-                    return 0
-
-                lax.fori_loop(1, 8, arrived, 0)
+                seven = self.r4.at[pl.ds(0, 7), at]
+                self.wait(seven, seven, 4, 4, send=False)
                 self.r4[mine, at, :] = self.a3[at, :]
                 total = self.r4[0, at, :].astype(F32)
                 for z in range(1, 8):
@@ -410,8 +393,8 @@
 
             @pl.when(self.holds(k))
             def _():
-                for s in range(1, R):
-                    self.fifth(k, s).wait_send()
+                seven = self.r4.at[pl.ds(0, 7), self.piece(k)]
+                self.wait(seven, seven, 6, 5 + k, recv=False)
 
             @pl.when(self.away(k))
             def _():
@@ -427,11 +410,11 @@
 
 
 def block_kernel(
-    x_ref, g_ref, w_ref, aw,
+    x_hbm, g_hbm, w_hbm, aw_hbm,
     dx, dconv, dattn,
-    xe, ae, hid, kt, joined, gpad, gt, mpad, mt, pt, gm,
+    xe, ae, hid, w_ref, kt, aw, joined, gpad, gt, mpad, mt, pt, gm,
     xc, ac, ge, uc, pre, pc, g1,
-    gs, gr, ms, mr, ps, pr, hs, hr, ks, kr,
+    gs, gr, ms, mr, ps, pr, hs, hr, ks, kr, ls,
     *bufs,
 ):
     tm, rows = lax.axis_index("tm"), lax.axis_index("rows")
@@ -439,29 +422,40 @@
     down = {"rows": lax.rem(rows + 1, R)}
     top, bottom = rows == 0, rows == R - 1
     work, bufs = bufs[:10], bufs[10:]
-    early = Reduction(EARLY, 48, bufs[:15], tm, rows)
-    late = Reduction(LATE, 48, bufs[15:], tm, rows)
+    attn = Reduction(2, 1, bufs[:13], tm, rows)
+    early = Reduction(4, 2, bufs[13:26], tm, rows)
+    late = Reduction(5, 3, bufs[26:], tm, rows)
     g_bufs, m_bufs, p_bufs = (gpad, gt, gs, gr), (mpad, mt, ms, mr), (pt, gm, ps, pr)
 
-    gpad[0, 0:10] = g_ref[0:1].reshape(10, PIX, C)
-    gpad[0, 10:30] = g_ref[4:6].reshape(20, PIX, C)
-    gpad[1, 0:30] = g_ref[1:4].reshape(30, PIX, C)
+    loads = [
+        pltpu.make_async_copy(x_hbm, xe.at[pl.ds(2, NR)], ls.at[0]),
+        pltpu.make_async_copy(g_hbm.at[pl.ds(0, 10)], gpad.at[0, pl.ds(0, 10)], ls.at[1]),
+        pltpu.make_async_copy(g_hbm.at[pl.ds(40, 20)], gpad.at[0, pl.ds(10, 20)], ls.at[2]),
+        pltpu.make_async_copy(g_hbm.at[pl.ds(10, 30)], gpad.at[1, pl.ds(0, 30)], ls.at[3]),
+        pltpu.make_async_copy(w_hbm, w_ref, ls.at[4]),
+        pltpu.make_async_copy(aw_hbm, aw, ls.at[5]),
+    ]
+    for load in loads:
+        load.start()
     for half in range(2):
         gpad[half, 30:32] = jnp.zeros((2, PIX, C), BF16)
         mpad[half, 30:32] = jnp.zeros((2, PIX, C), BF16)
     barrier(tm, rows)
-    to_up = remote(x_ref.at[pl.ds(0, 2)], xe.at[pl.ds(NR + 2, 2)], hs.at[0], hr.at[0], up)
-    to_down = remote(x_ref.at[pl.ds(NR - 2, 2)], xe.at[pl.ds(0, 2)], hs.at[1], hr.at[1], down)
+    loads[0].wait()
+    to_up = remote(xe.at[pl.ds(2, 2)], xe.at[pl.ds(NR + 2, 2)], hs.at[0], hr.at[0], up)
+    to_down = remote(xe.at[pl.ds(NR, 2)], xe.at[pl.ds(0, 2)], hs.at[1], hr.at[1], down)
     to_up.start()
     to_down.start()
+    for load in loads[1:4]:
+        load.wait()
     spread_start(g_bufs, 0, tm)
-    xe[2 : NR + 2] = x_ref[...]
     fill(xe, xc, 2, NR, True)
 
     def keep(first, hidden):
         hid[first : first + hidden.shape[0]] = hidden
         ae[first : first + hidden.shape[0]] = (hidden * jax.nn.sigmoid(hidden)).astype(BF16)
 
+    loads[4].wait()
     keep(2, conv(xc, ((2, 4),), w_ref[0], True))
     spread_start(g_bufs, 1, tm)
     to_up.wait()
@@ -477,12 +471,12 @@
     zero_at(ae, slice(NR + 1, NR + 2), bottom)
     fill(ae, ac, 0, NR + 2, True)
     branch = conv(ac, ((0, 1), (4, 2)), w_ref[1], True)
-    mixed = jnp.concatenate([x_ref[0:1], x_ref[4:6]], axis=0).astype(F32) + branch
+    mixed = jnp.concatenate([xe[2:3], xe[6:8]], axis=0).astype(F32) + branch
     mpad[0, 0:30] = mixed.astype(BF16).reshape(30, PIX, C)
     spread_start(m_bufs, 0, tm)
-    mixed = x_ref[1:4].astype(F32) + conv(ac, ((1, 3),), w_ref[1], True)
+    mixed = xe[3:6].astype(F32) + conv(ac, ((1, 3),), w_ref[1], True)
     mpad[1, 0:30] = mixed.astype(BF16).reshape(30, PIX, C)
-    spread_start(m_bufs, 1, tm)
+    loads[5].wait()
     joined[...] = jnp.concatenate([aw[0], aw[1], aw[2]], axis=1)
 
     def turn(i, _):
@@ -500,16 +494,18 @@
         return 0
 
     lax.fori_loop(0, NR + 2, slopes, 0)
+    spread_wait(g_bufs, 0, tm)
+    spread_wait(g_bufs, 1, tm)
+    spread_start(m_bufs, 1, tm)
     for half in range(2):
-        spread_wait(g_bufs, half, tm)
         spread_wait(m_bufs, half, tm)
         attend(half, mt, gt, pt, aw, joined, work, UNROLL)
         spread_start(p_bufs, half, tm)
 
     gup, normed, att, gj = work[6:10]
     proj = tn(normed[...], gj[...])
-    early.pack(64, proj[:, 0:C], proj[:, C : 2 * C])
-    early.pack(80, proj[:, 2 * C : 3 * C], tn(att[...], gup[...]))
+    attn.send(0, proj[:, 0:C], proj[:, C : 2 * C])
+    attn.send(1, proj[:, 2 * C : 3 * C], tn(att[...], gup[...]))
 
     spread_wait(p_bufs, 0, tm)
     ge[2:3] = gm[0, 0:10].reshape(1, W, C)
@@ -526,6 +522,11 @@
 
     for a in range(3):
         g1[a] = tn(stacked(ae, ((a, 1), (a + 4, 2))), stacked(uc, ((2, 1), (6, 2))))
+    attn.after_core()
+
+    def one(k):
+        return g1[k // 3, :, (k % 3) * C : (k % 3 + 1) * C]
+
     spread_wait(p_bufs, 1, tm)
     ge[3:6] = gm[1, 0:30].reshape(3, W, C)
     far_up = remote(ge.at[3], ge.at[NR + 3], ks.at[2], kr.at[2], up)
@@ -535,13 +536,8 @@
     fill(ge, uc, 3, 3, False)
     for a in range(3):
         g1[a] += tn(stacked(ae, ((a + 1, 3),)), stacked(uc, ((3, 3),)))
-
-    def one(k):
-        return g1[k // 3, :, (k % 3) * C : (k % 3 + 1) * C]
-
-    for k in range(0, 8, 2):
-        early.pack(k * 8, one(k), one(k + 1))
-    early.start()
+        for j in ((0,), (1, 2), (3,))[a]:
+            early.send(j, one(2 * j), one(2 * j + 1))
 
     def back(first, act_grad):
         at = slice(first, first + act_grad.shape[0])
@@ -554,45 +550,45 @@
     fill(ge, uc, 1, 1, False)
     fill(ge, uc, NR + 2, 1, False)
     back(1, conv(uc, ((1, 6),), kt[1], False))
+    attn.after_second()
     early.after_core()
     fill(pre, pc, 1, NR, False)
-    g0 = [
-        tn(xe[a + 1 : a + 1 + NR].reshape(NR * W, C), pc[1 : NR + 1].reshape(NR * W, 3 * C))
-        for a in range(3)
-    ]
+    g0 = []
 
     def zero(k):
         return g0[k // 3][:, (k % 3) * C : (k % 3 + 1) * C]
 
-    for k in range(0, 8, 2):
-        late.pack(k * 8, zero(k), zero(k + 1))
-    late.pack(64, zero(8), one(8))
-    late.start()
-    early.after_second()
+    for a in range(3):
+        g0.append(
+            tn(xe[a + 1 : a + 1 + NR].reshape(NR * W, C), pc[1 : NR + 1].reshape(NR * W, 3 * C))
+        )
+        for j in ((0,), (1, 2), (3, 4))[a]:
+            late.send(j, zero(2 * j), zero(2 * j + 1) if j < 4 else one(8))
     far_up.wait()
     far_down.wait()
     zero_at(ge, slice(0, 1), top)
     zero_at(ge, slice(NR + 3, NR + 4), bottom)
     fill(ge, uc, 0, 1, False)
     fill(ge, uc, NR + 3, 1, False)
+    late.after_core()
+    attn.after_third()
     ends = conv(uc, ((0, 1), (7, 1)), kt[1], False)
     back(0, ends[0:1])
     back(7, ends[1:2])
     zero_at(pre, slice(0, 1), top)
     zero_at(pre, slice(NR + 1, NR + 2), bottom)
-    late.after_core()
-    early.after_third()
     fill(pre, pc, 0, 1, False)
     fill(pre, pc, NR + 1, 1, False)
-    dx[0:3] = (ge[2:5].astype(F32) + conv(pc, ((0, 3),), kt[0], False)).astype(BF16)
+    early.after_second()
+    attn.after_fourth()
+    dx[...] = (ge[2:8].astype(F32) + conv(pc, ((0, 6),), kt[0], False)).astype(BF16)
     late.after_second()
-    dx[3:6] = (ge[5:8].astype(F32) + conv(pc, ((3, 3),), kt[0], False)).astype(BF16)
+    early.after_third()
+    late.after_third()
     early.after_fourth()
-    late.after_third()
-    sums = early.finish()
-    dconv[1, 0:8] = sums[0:64].reshape(8, 8, C)
-    dattn[...] = sums[64:96].reshape(4, 8, C)
     late.after_fourth()
+    dattn[...] = attn.finish().reshape(4, 8, C)
+    dconv[1, 0:8] = early.finish().reshape(8, 8, C)
     sums = late.finish()
     dconv[0] = sums[0:72].reshape(9, 8, C)
     dconv[1, 8:9] = sums[72:80].reshape(1, 8, C)
@@ -602,6 +598,10 @@
     x[...] = a[...]
     y[...] = b[...]
     z[...] = c[...]
+
+
+def anywhere(count):
+    return [pl.BlockSpec(memory_space=pl.ANY)] * count
 
 
 def vmem(count):
@@ -622,7 +622,7 @@
 
 def per_device(frames_in, grad_out, conv_weight, attn_weight):
     x = frames_in.reshape(NR, W, C)
-    g = grad_out.reshape(NR, W, C)
+    g = grad_out.reshape(NR * W // PIX, PIX, C)
     w = conv_weight.reshape(2, 9 * C, C)
     spread = pltpu.VMEM((2, T, PIX, C), BF16)
     shapes = [
@@ -633,13 +633,15 @@
     outs = pl.pallas_call(
         block_kernel,
         out_shape=shapes,
-        in_specs=vmem(4),
+        in_specs=anywhere(4),
         out_specs=vmem(3),
         scratch_shapes=[
             pltpu.VMEM((NR + 4, W, C), BF16),
             pltpu.VMEM((NR + 2, W, C), BF16),
             pltpu.VMEM((NR + 2, W, C), F32),
             pltpu.VMEM((2, 9 * C, C), BF16),
+            pltpu.VMEM((2, 9 * C, C), BF16),
+            pltpu.VMEM((4, C, C), BF16),
             pltpu.VMEM((C, 3 * C), BF16),
             *[spread] * 6,
             pltpu.VMEM((NR + 4, W, 3 * C), BF16),
@@ -649,11 +651,12 @@
             pltpu.VMEM((NR + 2, W, C), BF16),
             pltpu.VMEM((NR + 2, W, 3 * C), BF16),
             pltpu.VMEM((3, C, 3 * C), F32),
-            *[dma(2, T)] * 6,
-            dma(2), dma(2), dma(4), dma(4),
+            *[dma(2)] * 6,
+            dma(2), dma(2), dma(4), dma(4), dma(6),
             *attend_buffers(),
-            *Reduction.buffers(EARLY, 48),
-            *Reduction.buffers(LATE, 48),
+            *Reduction.buffers(2, 1),
+            *Reduction.buffers(4, 2),
+            *Reduction.buffers(5, 3),
         ],
         compiler_params=params(1),
         name="block",

time: 103 us -> 91.4 us (0.89)
  Pallas kernels: 102 us -> 90.6 us
    pallas_call x1, Pallas kernels: 99.8 us -> 88.6 us  [per_device(): pl.pallas_call(block_kernel, out_shape=shapes, in_specs=anywhere(4), out_...]
where the time goes in v3:
time: 91.4 us; the launch traced here: 91.2 us
  Pallas kernels  90.6 us (99%)
    pallas_call x1, Pallas kernels, per_device(): pl.pallas_call(block_kernel, out_shape=shapes, in_specs=anywhere(4), out_...  88.6 us
    pallas_call x1, Pallas kernels, per_device(): pl.pallas_call(pass_kernel, out_shape=shapes, in_specs=vmem(3), out_specs...  1.95 us

profile of v3, /device:TPU:4, one launch (start us, length us, event | category | flops | bytes accessed | tf_op | source)
XLA Modules:
  0.0 91.2 jit_solution(10126507944257639765)
XLA Ops:
  0.6 88.6 %block.1 = (bf16[6,160,256]{2,1,0:T(8,128)(2,1)}, f32[2,9,8,256]{3,2,1,0:T(8,128)}, f32[4,8,256]{2,1,0:T(8,128)}) custom-call(bf16[6,160,256]{2,1,0:T(8,128)(2,1)} %bitcast.5, bf16[60,16,256]{2,1,0:T(8,128)(2,1)} %bitcast.6, bf16[2,2304,256]{2,1,0:T(8,128)(2,1)} %bitcast.4, bf16[4,256,256]{2,1,0:T(8,128)(2,1)} %aw_hbm.1), custom_call_target="tpu_custom_call" | custom-call | tf_op jit(solution)/shard_map/block/pallas_call | solution.py:633
  89.2 2.0 %hand_on.1 = (bf16[6,160,256]{2,1,0:T(8,128)(2,1)}, f32[2,9,8,256]{3,2,1,0:T(8,128)}, f32[4,8,256]{2,1,0:T(8,128)}) custom-call(bf16[6,160,256]{2,1,0:T(8,128)(2,1)} %get-tuple-element.9.a, f32[2,9,8,256]{3,2,1,0:T(8,128)} %get-tuple-element.10.b, f32[4,8,256]{2,1,0:T(8,128)} %get-tuple-element.11.c), custom_call_target="tpu_custom_call" | custom-call | tf_op jit(solution)/shard_map/hand_on/pallas_call | solution.py:664

commit v4 on v3

--- a/solution.py
+++ b/solution.py
@@ -216,15 +216,12 @@
 
 
 class Reduction:
-    count = 13
-
     @staticmethod
-    def buffers(pairs, xp):
+    def buffers(pairs, xp, joint):
         n, nx = pairs * 16, xp * 16
         ny = n - nx
         shapes = [
-            (pairs, 2, 16, 16),
-            (pairs, 16, 16),
+            *(() if joint else ((pairs, 2, 16, 16), (pairs, 16, 16))),
             (4, 4, nx), (4, 4, ny),
             (3, 4, nx), (3, 4, ny),
             (3, nx), (3, ny),
@@ -232,22 +229,25 @@
             (8, n),
             (n,),
         ]
-        return [pltpu.VMEM(s + (C,), BF16) for s in shapes] + [dma(pairs + 7), dma(pairs + 7)]
-
-    def __init__(self, pairs, xp, bufs, tm, rows):
-        self.pairs, self.xp = pairs, xp
+        return [pltpu.VMEM(s + (C,), BF16) for s in shapes] + [dma(7 if joint else pairs + 7)] * 2
+
+    def __init__(self, pairs, xp, joint, bufs, tm, rows):
+        self.pairs, self.xp, self.joint = pairs, xp, joint
+        self.skip = 0 if joint else pairs
+        if not joint:
+            self.packed, self.r1 = bufs[0:2]
+            bufs = bufs[2:]
         self.n, self.nx = pairs * 16, xp * 16
         self.cut = self.nx
-        self.packed, self.r1, self.ax1, self.ay1 = bufs[0:4]
-        self.rx2, self.ry2, self.rx3, self.ry3, self.a3, self.r4, self.out = bufs[4:11]
-        self.ss, self.rs = bufs[11:13]
+        self.ax1, self.ay1, self.rx2, self.ry2, self.rx3, self.ry3 = bufs[0:6]
+        self.a3, self.r4, self.out, self.ss, self.rs = bufs[6:11]
         self.core, self.y, self.z_hi = lax.rem(tm, 2), lax.rem(tm // 2, 4), tm // 8
         self.x, self.z_lo = lax.rem(rows, 4), rows // 4
         self.tm, self.rows = tm, rows
 
     def copy(self, src, dst, s, r, device):
         return remote(
-            src, dst, self.ss.at[self.pairs + s], self.rs.at[self.pairs + r], device
+            src, dst, self.ss.at[self.skip + s], self.rs.at[self.skip + r], device
         )
 
     def tm_at(self, z_hi, y):
@@ -262,11 +262,30 @@
             self.packed.at[j, 1 - self.core], self.r1.at[j], self.ss.at[j], self.rs.at[j], other
         )
 
+    def place(self, j):
+        in_x = j < self.xp
+        return self.ax1 if in_x else self.ay1, pl.ds((j if in_x else j - self.xp) * 16, 16)
+
+    def send_on(self, j):
+        if j == self.xp - 1 or j == self.pairs - 1:
+            for s in (1, 2, 3):
+                (self.second_x if j < self.xp else self.second_y)(s).start()
+
     def send(self, j, upper, lower):
-        for t in range(T):
+        for t in range(T // 2 if self.joint else T):
             both = jnp.concatenate([upper[t * 8 : t * 8 + 8], lower[t * 8 : t * 8 + 8]], axis=0)
-            self.packed[j, t % 2, t // 2] = both.astype(BF16)
-        self.first(j).start()
+            core, t = (0, t) if self.joint else (t % 2, t // 2)
+            z, y = t // 4, t % 4
+            k = z * 4 + y if j < self.xp else y * 4 + z
+            if self.joint:
+                to, at = self.place(j)
+                to[k // 4, k % 4, at, :] = both.astype(BF16)
+            else:
+                self.packed[j, core, k] = both.astype(BF16)
+        if self.joint:
+            self.send_on(j)
+        else:
+            self.first(j).start()
 
     def second_x(self, s):
         x = lax.rem(self.x + s, 4)
@@ -318,24 +337,10 @@
     def after_core(self):
         for j in range(self.pairs):
             self.first(j).wait()
-            in_x = j < self.xp
-            at = pl.ds((j if in_x else j - self.xp) * 16, 16)
-
-            def add(k, _):
-                z, y = k // 4, lax.rem(k, 4)
-                total = self.packed[j, self.core, k].astype(F32) + self.r1[j, k].astype(F32)
-                if in_x:
-                    self.ax1[z, y, at, :] = total.astype(BF16)
-                else:
-                    self.ay1[y, z, at, :] = total.astype(BF16)
-                return 0
-
-            lax.fori_loop(0, 16, add, 0, unroll=4)
-            if j == self.xp - 1:
-                for s in (1, 2, 3):
-                    self.second_x(s).start()
-        for s in (1, 2, 3):
-            self.second_y(s).start()
+            to, at = self.place(j)
+            total = self.packed[j, self.core].astype(F32) + self.r1[j].astype(F32)
+            to[:, :, at, :] = total.astype(BF16).reshape(4, 4, 16, C)
+            self.send_on(j)
 
     def after_second(self):
         for a, r, me, i, go in (
@@ -343,11 +348,10 @@
             (self.ay1, self.ry2, self.y, 1, self.third_y),
         ):
             self.wait(r, r, i, i)
-            for j in range(4):
-                total = a[me, j].astype(F32)
-                for s in range(3):
-                    total += r[s, j].astype(F32)
-                a[me, j] = total.astype(BF16)
+            total = a[me].astype(F32)
+            for s in range(3):
+                total += r[s].astype(F32)
+            a[me] = total.astype(BF16)
             for s in (1, 2, 3):
                 go(s).start()
 
@@ -413,8 +417,8 @@
     x_hbm, g_hbm, w_hbm, aw_hbm,
     dx, dconv, dattn,
     xe, ae, hid, w_ref, kt, aw, joined, gpad, gt, mpad, mt, pt, gm,
-    xc, ac, ge, uc, pre, pc, g1,
-    gs, gr, ms, mr, ps, pr, hs, hr, ks, kr, ls,
+    xc, ac, ge, uc, pre, pc, g1, xt, at0, at1, xs, as0, as1, u0, s0, u1, s1,
+    gs, gr, ms, mr, ps, pr, hs, hr, ks, kr, ls, ts, tr,
     *bufs,
 ):
     tm, rows = lax.axis_index("tm"), lax.axis_index("rows")
@@ -422,9 +426,11 @@
     down = {"rows": lax.rem(rows + 1, R)}
     top, bottom = rows == 0, rows == R - 1
     work, bufs = bufs[:10], bufs[10:]
-    attn = Reduction(2, 1, bufs[:13], tm, rows)
-    early = Reduction(4, 2, bufs[13:26], tm, rows)
-    late = Reduction(5, 3, bufs[26:], tm, rows)
+    attn = Reduction(2, 1, False, bufs[:13], tm, rows)
+    early = Reduction(4, 2, True, bufs[13:24], tm, rows)
+    late = Reduction(5, 3, True, bufs[24:], tm, rows)
+    core = lax.rem(tm, 2)
+    twin = {"tm": tm + 1 - 2 * core}
     g_bufs, m_bufs, p_bufs = (gpad, gt, gs, gr), (mpad, mt, ms, mr), (pt, gm, ps, pr)
 
     loads = [
@@ -476,6 +482,7 @@
     spread_start(m_bufs, 0, tm)
     mixed = xe[3:6].astype(F32) + conv(ac, ((1, 3),), w_ref[1], True)
     mpad[1, 0:30] = mixed.astype(BF16).reshape(30, PIX, C)
+    spread_wait(g_bufs, 0, tm)
     loads[5].wait()
     joined[...] = jnp.concatenate([aw[0], aw[1], aw[2]], axis=1)
 
@@ -494,7 +501,40 @@
         return 0
 
     lax.fori_loop(0, NR + 2, slopes, 0)
-    spread_wait(g_bufs, 0, tm)
+
+    def flip(to, a, b, pieces, depth):
+        rows_in = [p.reshape(-1, C).astype(F32) for p in pieces]
+        short = depth - sum(p.shape[0] for p in rows_in)
+        flat = jnp.concatenate(rows_in + [jnp.zeros((short, C), F32)], axis=0).T
+        flat = flat.reshape(16, 2, 8, depth)
+        for c in range(2):
+            to[c, a, b * 128 : (b + 1) * 128, :] = flat[:, c].reshape(128, depth).astype(BF16)
+
+    def flips(a, _):
+        for b in range(3):
+            at = pl.ds(b * C, C)
+            flip(xt, a, b, [xc[pl.ds(a + 1, NR), :, at]], 1024)
+            flip(at0, a, b, [ac[pl.ds(a, 1), :, at], ac[pl.ds(a + 4, 2), :, at]], 512)
+            flip(at1, a, b, [ac[pl.ds(a + 1, 3), :, at]], 512)
+        return 0
+
+    lax.fori_loop(0, 3, flips, 0)
+    swaps = [
+        remote(src.at[1 - core], dst, ts.at[k], tr.at[k], twin)
+        for k, (src, dst) in enumerate(((at0, as0), (at1, as1), (xt, xs)))
+    ]
+    for swap in swaps:
+        swap.start()
+    for buf in (u1, s1):
+        buf[:, 480:512] = jnp.zeros((2, 32, C), BF16)
+    for buf in (u0, s0):
+        buf[960:1024] = jnp.zeros((64, C), BF16)
+    full = pl.ds(0, 480)
+    u_swaps = [
+        remote(u1.at[0, full], s1.at[0, full], ts.at[3], tr.at[3], twin),
+        remote(u1.at[1, full], s1.at[1, full], ts.at[4], tr.at[4], twin),
+        remote(u0.at[pl.ds(0, 960)], s0.at[pl.ds(0, 960)], ts.at[5], tr.at[5], twin),
+    ]
     spread_wait(g_bufs, 1, tm)
     spread_start(m_bufs, 1, tm)
     for half in range(2):
@@ -510,6 +550,8 @@
     spread_wait(p_bufs, 0, tm)
     ge[2:3] = gm[0, 0:10].reshape(1, W, C)
     ge[6:8] = gm[0, 10:30].reshape(2, W, C)
+    u1[0, 0:480] = gm[0, 0:30].reshape(480, C)
+    u_swaps[0].start()
     near_up = remote(ge.at[2], ge.at[NR + 2], ks.at[0], kr.at[0], up)
     near_down = remote(ge.at[NR + 1], ge.at[1], ks.at[1], kr.at[1], down)
     near_up.start()
@@ -517,27 +559,28 @@
     fill(ge, uc, 2, 1, False)
     fill(ge, uc, 6, 2, False)
 
-    def stacked(ref, runs):
-        return jnp.concatenate([ref[s : s + n].reshape(n * W, ref.shape[2]) for s, n in runs], axis=0)
-
+    def times(a, b):
+        return jnp.dot(a, b, preferred_element_type=F32)
+
+    for swap in swaps:
+        swap.wait()
+    u_swaps[0].wait()
     for a in range(3):
-        g1[a] = tn(stacked(ae, ((a, 1), (a + 4, 2))), stacked(uc, ((2, 1), (6, 2))))
+        g1[a] = times(at0[core, a], u1[0]) + times(as0[a], s1[0])
     attn.after_core()
 
     def one(k):
-        return g1[k // 3, :, (k % 3) * C : (k % 3 + 1) * C]
+        return g1[k // 3, (k % 3) * 128 : (k % 3 + 1) * 128, :]
 
     spread_wait(p_bufs, 1, tm)
     ge[3:6] = gm[1, 0:30].reshape(3, W, C)
+    u1[1, 0:480] = gm[1, 0:30].reshape(480, C)
+    u_swaps[1].start()
     far_up = remote(ge.at[3], ge.at[NR + 3], ks.at[2], kr.at[2], up)
     far_down = remote(ge.at[NR], ge.at[0], ks.at[3], kr.at[3], down)
     far_up.start()
     far_down.start()
     fill(ge, uc, 3, 3, False)
-    for a in range(3):
-        g1[a] += tn(stacked(ae, ((a + 1, 3),)), stacked(uc, ((3, 3),)))
-        for j in ((0,), (1, 2), (3,))[a]:
-            early.send(j, one(2 * j), one(2 * j + 1))
 
     def back(first, act_grad):
         at = slice(first, first + act_grad.shape[0])
@@ -550,41 +593,43 @@
     fill(ge, uc, 1, 1, False)
     fill(ge, uc, NR + 2, 1, False)
     back(1, conv(uc, ((1, 6),), kt[1], False))
-    attn.after_second()
-    early.after_core()
-    fill(pre, pc, 1, NR, False)
+    u0[0:960] = pre[1 : NR + 1].reshape(960, C)
+    u_swaps[2].start()
+    u_swaps[1].wait()
+    for a in range(3):
+        g1[a] += times(at1[core, a], u1[1]) + times(as1[a], s1[1])
+        for j in ((0,), (1, 2), (3,))[a]:
+            early.send(j, one(2 * j), one(2 * j + 1))
     g0 = []
 
     def zero(k):
-        return g0[k // 3][:, (k % 3) * C : (k % 3 + 1) * C]
-
+        return g0[k // 3][(k % 3) * 128 : (k % 3 + 1) * 128]
+
+    u_swaps[2].wait()
     for a in range(3):
-        g0.append(
-            tn(xe[a + 1 : a + 1 + NR].reshape(NR * W, C), pc[1 : NR + 1].reshape(NR * W, 3 * C))
-        )
+        g0.append(times(xt[core, a], u0[...]) + times(xs[a], s0[...]))
         for j in ((0,), (1, 2), (3, 4))[a]:
             late.send(j, zero(2 * j), zero(2 * j + 1) if j < 4 else one(8))
+    attn.after_second()
     far_up.wait()
     far_down.wait()
     zero_at(ge, slice(0, 1), top)
     zero_at(ge, slice(NR + 3, NR + 4), bottom)
     fill(ge, uc, 0, 1, False)
     fill(ge, uc, NR + 3, 1, False)
-    late.after_core()
-    attn.after_third()
     ends = conv(uc, ((0, 1), (7, 1)), kt[1], False)
     back(0, ends[0:1])
     back(7, ends[1:2])
     zero_at(pre, slice(0, 1), top)
     zero_at(pre, slice(NR + 1, NR + 2), bottom)
-    fill(pre, pc, 0, 1, False)
-    fill(pre, pc, NR + 1, 1, False)
+    fill(pre, pc, 0, NR + 2, False)
     early.after_second()
-    attn.after_fourth()
     dx[...] = (ge[2:8].astype(F32) + conv(pc, ((0, 6),), kt[0], False)).astype(BF16)
+    attn.after_third()
     late.after_second()
     early.after_third()
     late.after_third()
+    attn.after_fourth()
     early.after_fourth()
     late.after_fourth()
     dattn[...] = attn.finish().reshape(4, 8, C)
@@ -594,10 +639,17 @@
     dconv[1, 8:9] = sums[72:80].reshape(1, 8, C)
 
 
-def pass_kernel(a, b, c, x, y, z):
-    x[...] = a[...]
-    y[...] = b[...]
-    z[...] = c[...]
+def pass_kernel(a, b, c, x, y, z, va, vb, vc, sems):
+    trips = [(a.at[i], va.at[i], x.at[i]) for i in range(NR)] + [(b, vb, y), (c, vc, z)]
+    into = [pltpu.make_async_copy(s, v, sems.at[k]) for k, (s, v, _) in enumerate(trips)]
+    out = [pltpu.make_async_copy(v, d, sems.at[8 + k]) for k, (_, v, d) in enumerate(trips)]
+    for copy in into:
+        copy.start()
+    for k in range(8):
+        into[k].wait()
+        out[k].start()
+    for copy in out:
+        copy.wait()
 
 
 def anywhere(count):
@@ -650,13 +702,23 @@
             pltpu.VMEM((NR + 4, W, 3 * C), BF16),
             pltpu.VMEM((NR + 2, W, C), BF16),
             pltpu.VMEM((NR + 2, W, 3 * C), BF16),
-            pltpu.VMEM((3, C, 3 * C), F32),
+            pltpu.VMEM((3, 384, C), F32),
+            pltpu.VMEM((2, 3, 384, 1024), BF16),
+            pltpu.VMEM((2, 3, 384, 512), BF16),
+            pltpu.VMEM((2, 3, 384, 512), BF16),
+            pltpu.VMEM((3, 384, 1024), BF16),
+            pltpu.VMEM((3, 384, 512), BF16),
+            pltpu.VMEM((3, 384, 512), BF16),
+            pltpu.VMEM((1024, C), BF16),
+            pltpu.VMEM((1024, C), BF16),
+            pltpu.VMEM((2, 512, C), BF16),
+            pltpu.VMEM((2, 512, C), BF16),
             *[dma(2)] * 6,
-            dma(2), dma(2), dma(4), dma(4), dma(6),
+            dma(2), dma(2), dma(4), dma(4), dma(6), dma(6), dma(6),
             *attend_buffers(),
-            *Reduction.buffers(2, 1),
-            *Reduction.buffers(4, 2),
-            *Reduction.buffers(5, 3),
+            *Reduction.buffers(2, 1, False),
+            *Reduction.buffers(4, 2, True),
+            *Reduction.buffers(5, 3, True),
         ],
         compiler_params=params(1),
         name="block",
@@ -664,8 +726,9 @@
     dx, dconv, dattn = pl.pallas_call(
         pass_kernel,
         out_shape=shapes,
-        in_specs=vmem(3),
-        out_specs=vmem(3),
+        in_specs=anywhere(3),
+        out_specs=anywhere(3),
+        scratch_shapes=[*[pltpu.VMEM(s.shape, s.dtype) for s in shapes], dma(16)],
         compiler_params=params(),
         name="hand_on",
     )(*outs)

time: 91.4 us -> 89.4 us (0.978)
  Pallas kernels: 90.6 us -> 88.3 us
    pallas_call x1, Pallas kernels: 88.6 us -> 86.4 us  [per_device(): pl.pallas_call(block_kernel, out_shape=shapes, in_specs=anywhere(4), out_...]
where the time goes in v4:
time: 89.4 us; the launch traced here: 89.1 us
  Pallas kernels  88.3 us (99%)
    pallas_call x1, Pallas kernels, per_device(): pl.pallas_call(block_kernel, out_shape=shapes, in_specs=anywhere(4), out_...  86.4 us
    pallas_call x1, Pallas kernels, per_device(): pl.pallas_call(pass_kernel, out_shape=shapes, in_specs=anywhere(3), out_s...  1.95 us

profile of v4, /device:TPU:4, one launch (start us, length us, event | category | flops | bytes accessed | tf_op | source)
XLA Modules:
  0.0 89.1 jit_solution(16311975233986722854)
XLA Ops:
  0.6 86.4 %block.1 = (bf16[6,160,256]{2,1,0:T(8,128)(2,1)}, f32[2,9,8,256]{3,2,1,0:T(8,128)}, f32[4,8,256]{2,1,0:T(8,128)}) custom-call(bf16[6,160,256]{2,1,0:T(8,128)(2,1)} %bitcast.5, bf16[60,16,256]{2,1,0:T(8,128)(2,1)} %bitcast.6, bf16[2,2304,256]{2,1,0:T(8,128)(2,1)} %bitcast.4, bf16[4,256,256]{2,1,0:T(8,128)(2,1)} %aw_hbm.1), custom_call_target="tpu_custom_call" | custom-call | tf_op jit(solution)/shard_map/block/pallas_call | solution.py:685
  87.0 1.9 %hand_on.1 = (bf16[6,160,256]{2,1,0:T(8,128)(2,1)}, f32[2,9,8,256]{3,2,1,0:T(8,128)}, f32[4,8,256]{2,1,0:T(8,128)}) custom-call(bf16[6,160,256]{2,1,0:T(8,128)(2,1)} %get-tuple-element.9.a, f32[2,9,8,256]{3,2,1,0:T(8,128)} %get-tuple-element.10.b, f32[4,8,256]{2,1,0:T(8,128)} %get-tuple-element.11.c), custom_call_target="tpu_custom_call" | custom-call | tf_op jit(solution)/shard_map/hand_on/pallas_call | solution.py:726

commit v5 on v4

--- a/solution.py
+++ b/solution.py
@@ -13,6 +13,8 @@
 NR, W, C = 6, 160, 256
 PIX = 16
 UNROLL = 4
+IDLE = ((0, 10), (20, 30))
+RUNS = (((1, 0, 9), (11, 9, 21)), ((0, 0, 20), (21, 20, 9), (31, 29, 1)))
 F32, BF16 = jnp.float32, jnp.bfloat16
 MESH = pl.DeviceIdType.MESH
 VMEM_LIMIT = 60 * 1024 * 1024
@@ -48,29 +50,66 @@
     )
 
 
-def spread_start(bufs, half, tm):
+def busy(half, device):
+    return jnp.logical_and(device != IDLE[half][0], device != IDLE[half][1])
+
+
+def spread_start(bufs, half, tm, back=False):
     src, dst, ss, rs = bufs
 
     def go(s, _):
         peer = lax.rem(tm + s, T)
-        remote(
-            src.at[half, peer], dst.at[half, tm], ss.at[half], rs.at[half], {"tm": peer}
-        ).start()
+
+        @pl.when(busy(half, tm if back else peer))
+        def _():
+            remote(
+                src.at[half, peer], dst.at[half, tm], ss.at[half], rs.at[half], {"tm": peer}
+            ).start()
+
         return 0
 
     lax.fori_loop(1, T, go, 0)
     dst[half, tm] = src[half, tm]
 
 
-def spread_wait(bufs, half, tm):
+def spread_wait(bufs, half, tm, back=False):
     src, dst, ss, rs = bufs
-    every = pl.ds(0, T - 1)
-    copy = remote(
-        src.at[half, every], dst.at[half, every], ss.at[half], rs.at[half],
-        {"tm": lax.rem(tm + 1, T)},
-    )
-    copy.wait_send()
-    copy.wait_recv()
+
+    def chunks(count):
+        some = pl.ds(0, count)
+        return remote(
+            src.at[half, some], dst.at[half, some], ss.at[half], rs.at[half],
+            {"tm": lax.rem(tm + 1, T)},
+        )
+
+    working = busy(half, tm)
+
+    @pl.when(working)
+    def _():
+        if back:
+            chunks(31).wait_send()
+            chunks(29).wait_recv()
+        else:
+            chunks(29).wait_send()
+            chunks(31).wait_recv()
+
+    @pl.when(jnp.logical_not(working))
+    def _():
+        if back:
+            chunks(30).wait_recv()
+        else:
+            chunks(30).wait_send()
+            dst[half] = jnp.zeros((T, PIX, C), BF16)
+
+
+def spread_out(to, half, chunks):
+    for device, first, count in RUNS[half]:
+        to[half, device : device + count] = chunks[first : first + count]
+
+
+def gathered(ref, half):
+    runs = [ref[half, device : device + count] for device, _, count in RUNS[half]]
+    return jnp.concatenate(runs, axis=0).reshape(30 * PIX, C)
 
 
 def shifts(row):
@@ -435,24 +474,30 @@
 
     loads = [
         pltpu.make_async_copy(x_hbm, xe.at[pl.ds(2, NR)], ls.at[0]),
-        pltpu.make_async_copy(g_hbm.at[pl.ds(0, 10)], gpad.at[0, pl.ds(0, 10)], ls.at[1]),
-        pltpu.make_async_copy(g_hbm.at[pl.ds(40, 20)], gpad.at[0, pl.ds(10, 20)], ls.at[2]),
-        pltpu.make_async_copy(g_hbm.at[pl.ds(10, 30)], gpad.at[1, pl.ds(0, 30)], ls.at[3]),
-        pltpu.make_async_copy(w_hbm, w_ref, ls.at[4]),
-        pltpu.make_async_copy(aw_hbm, aw, ls.at[5]),
+        *(
+            pltpu.make_async_copy(
+                g_hbm.at[pl.ds(first, count)], gpad.at[half, pl.ds(device, count)], ls.at[1 + k]
+            )
+            for k, (half, device, first, count) in enumerate(
+                ((0, 1, 0, 9), (0, 11, 9, 1), (0, 12, 40, 20), (1, 0, 10, 20), (1, 21, 30, 9), (1, 31, 39, 1))
+            )
+        ),
+        pltpu.make_async_copy(w_hbm, w_ref, ls.at[7]),
+        pltpu.make_async_copy(aw_hbm, aw, ls.at[8]),
     ]
     for load in loads:
         load.start()
     for half in range(2):
-        gpad[half, 30:32] = jnp.zeros((2, PIX, C), BF16)
-        mpad[half, 30:32] = jnp.zeros((2, PIX, C), BF16)
+        for device in IDLE[half]:
+            gpad[half, device] = jnp.zeros((PIX, C), BF16)
+            mpad[half, device] = jnp.zeros((PIX, C), BF16)
     barrier(tm, rows)
     loads[0].wait()
     to_up = remote(xe.at[pl.ds(2, 2)], xe.at[pl.ds(NR + 2, 2)], hs.at[0], hr.at[0], up)
     to_down = remote(xe.at[pl.ds(NR, 2)], xe.at[pl.ds(0, 2)], hs.at[1], hr.at[1], down)
     to_up.start()
     to_down.start()
-    for load in loads[1:4]:
+    for load in loads[1:7]:
         load.wait()
     spread_start(g_bufs, 0, tm)
     fill(xe, xc, 2, NR, True)
@@ -461,7 +506,7 @@
         hid[first : first + hidden.shape[0]] = hidden
         ae[first : first + hidden.shape[0]] = (hidden * jax.nn.sigmoid(hidden)).astype(BF16)
 
-    loads[4].wait()
+    loads[7].wait()
     keep(2, conv(xc, ((2, 4),), w_ref[0], True))
     spread_start(g_bufs, 1, tm)
     to_up.wait()
@@ -478,12 +523,12 @@
     fill(ae, ac, 0, NR + 2, True)
     branch = conv(ac, ((0, 1), (4, 2)), w_ref[1], True)
     mixed = jnp.concatenate([xe[2:3], xe[6:8]], axis=0).astype(F32) + branch
-    mpad[0, 0:30] = mixed.astype(BF16).reshape(30, PIX, C)
+    spread_out(mpad, 0, mixed.astype(BF16).reshape(30, PIX, C))
     spread_start(m_bufs, 0, tm)
     mixed = xe[3:6].astype(F32) + conv(ac, ((1, 3),), w_ref[1], True)
-    mpad[1, 0:30] = mixed.astype(BF16).reshape(30, PIX, C)
+    spread_out(mpad, 1, mixed.astype(BF16).reshape(30, PIX, C))
     spread_wait(g_bufs, 0, tm)
-    loads[5].wait()
+    loads[8].wait()
     joined[...] = jnp.concatenate([aw[0], aw[1], aw[2]], axis=1)
 
     def turn(i, _):
@@ -540,17 +585,18 @@
     for half in range(2):
         spread_wait(m_bufs, half, tm)
         attend(half, mt, gt, pt, aw, joined, work, UNROLL)
-        spread_start(p_bufs, half, tm)
+        spread_start(p_bufs, half, tm, True)
 
     gup, normed, att, gj = work[6:10]
     proj = tn(normed[...], gj[...])
     attn.send(0, proj[:, 0:C], proj[:, C : 2 * C])
     attn.send(1, proj[:, 2 * C : 3 * C], tn(att[...], gup[...]))
 
-    spread_wait(p_bufs, 0, tm)
-    ge[2:3] = gm[0, 0:10].reshape(1, W, C)
-    ge[6:8] = gm[0, 10:30].reshape(2, W, C)
-    u1[0, 0:480] = gm[0, 0:30].reshape(480, C)
+    spread_wait(p_bufs, 0, tm, True)
+    outer = gathered(gm, 0)
+    ge[2:3] = outer[0:W].reshape(1, W, C)
+    ge[6:8] = outer[W:].reshape(2, W, C)
+    u1[0, 0:480] = outer
     u_swaps[0].start()
     near_up = remote(ge.at[2], ge.at[NR + 2], ks.at[0], kr.at[0], up)
     near_down = remote(ge.at[NR + 1], ge.at[1], ks.at[1], kr.at[1], down)
@@ -572,9 +618,10 @@
     def one(k):
         return g1[k // 3, (k % 3) * 128 : (k % 3 + 1) * 128, :]
 
-    spread_wait(p_bufs, 1, tm)
-    ge[3:6] = gm[1, 0:30].reshape(3, W, C)
-    u1[1, 0:480] = gm[1, 0:30].reshape(480, C)
+    spread_wait(p_bufs, 1, tm, True)
+    inner = gathered(gm, 1)
+    ge[3:6] = inner.reshape(3, W, C)
+    u1[1, 0:480] = inner
     u_swaps[1].start()
     far_up = remote(ge.at[3], ge.at[NR + 3], ks.at[2], kr.at[2], up)
     far_down = remote(ge.at[NR], ge.at[0], ks.at[3], kr.at[3], down)
@@ -714,7 +761,7 @@
             pltpu.VMEM((2, 512, C), BF16),
             pltpu.VMEM((2, 512, C), BF16),
             *[dma(2)] * 6,
-            dma(2), dma(2), dma(4), dma(4), dma(6), dma(6), dma(6),
+            dma(2), dma(2), dma(4), dma(4), dma(9), dma(6), dma(6),
             *attend_buffers(),
             *Reduction.buffers(2, 1, False),
             *Reduction.buffers(4, 2, True),

time: 89.4 us -> 85.5 us (0.956)
  Pallas kernels: 88.3 us -> 84.6 us
    pallas_call x1, Pallas kernels: 86.4 us -> 82.7 us  [per_device(): pl.pallas_call(block_kernel, out_shape=shapes, in_specs=anywhere(4), out_...]
where the time goes in v5:
time: 85.5 us; the launch traced here: 85.4 us
  Pallas kernels  84.6 us (99%)
    pallas_call x1, Pallas kernels, per_device(): pl.pallas_call(block_kernel, out_shape=shapes, in_specs=anywhere(4), out_...  82.7 us
    pallas_call x1, Pallas kernels, per_device(): pl.pallas_call(pass_kernel, out_shape=shapes, in_specs=anywhere(3), out_s...  1.95 us

profile of v5, /device:TPU:4, one launch (start us, length us, event | category | flops | bytes accessed | tf_op | source)
XLA Modules:
  0.0 85.4 jit_solution(8950152243639668180)
XLA Ops:
  0.6 82.7 %block.1 = (bf16[6,160,256]{2,1,0:T(8,128)(2,1)}, f32[2,9,8,256]{3,2,1,0:T(8,128)}, f32[4,8,256]{2,1,0:T(8,128)}) custom-call(bf16[6,160,256]{2,1,0:T(8,128)(2,1)} %bitcast.5, bf16[60,16,256]{2,1,0:T(8,128)(2,1)} %bitcast.6, bf16[2,2304,256]{2,1,0:T(8,128)(2,1)} %bitcast.4, bf16[4,256,256]{2,1,0:T(8,128)(2,1)} %aw_hbm.1), custom_call_target="tpu_custom_call" | custom-call | tf_op jit(solution)/shard_map/block/pallas_call | solution.py:732
  83.3 1.9 %hand_on.1 = (bf16[6,160,256]{2,1,0:T(8,128)(2,1)}, f32[2,9,8,256]{3,2,1,0:T(8,128)}, f32[4,8,256]{2,1,0:T(8,128)}) custom-call(bf16[6,160,256]{2,1,0:T(8,128)(2,1)} %get-tuple-element.9.a, f32[2,9,8,256]{3,2,1,0:T(8,128)} %get-tuple-element.10.b, f32[4,8,256]{2,1,0:T(8,128)} %get-tuple-element.11.c), custom_call_target="tpu_custom_call" | custom-call | tf_op jit(solution)/shard_map/hand_on/pallas_call | solution.py:773

commit v6 on v5

--- a/solution.py
+++ b/solution.py
@@ -500,6 +500,7 @@
     for load in loads[1:7]:
         load.wait()
     spread_start(g_bufs, 0, tm)
+    spread_start(g_bufs, 1, tm)
     fill(xe, xc, 2, NR, True)
 
     def keep(first, hidden):
@@ -508,7 +509,6 @@
 
     loads[7].wait()
     keep(2, conv(xc, ((2, 4),), w_ref[0], True))
-    spread_start(g_bufs, 1, tm)
     to_up.wait()
     to_down.wait()
     zero_at(xe, slice(0, 2), top)
@@ -568,8 +568,6 @@
         remote(src.at[1 - core], dst, ts.at[k], tr.at[k], twin)
         for k, (src, dst) in enumerate(((at0, as0), (at1, as1), (xt, xs)))
     ]
-    for swap in swaps:
-        swap.start()
     for buf in (u1, s1):
         buf[:, 480:512] = jnp.zeros((2, 32, C), BF16)
     for buf in (u0, s0):
@@ -582,6 +580,8 @@
     ]
     spread_wait(g_bufs, 1, tm)
     spread_start(m_bufs, 1, tm)
+    for swap in swaps:
+        swap.start()
     for half in range(2):
         spread_wait(m_bufs, half, tm)
         attend(half, mt, gt, pt, aw, joined, work, UNROLL)

time: 85.5 us -> 85.4 us (level)
  no operation moved by 1% of the time
where the time goes in v6:
time: 85.4 us; the launch traced here: 85.3 us
  Pallas kernels  84.5 us (99%)
    pallas_call x1, Pallas kernels, per_device(): pl.pallas_call(block_kernel, out_shape=shapes, in_specs=anywhere(4), out_...  82.5 us
    pallas_call x1, Pallas kernels, per_device(): pl.pallas_call(pass_kernel, out_shape=shapes, in_specs=anywhere(3), out_s...  1.95 us

profile of v6, /device:TPU:4, one launch (start us, length us, event | category | flops | bytes accessed | tf_op | source)
XLA Modules:
  0.0 85.3 jit_solution(13516524457828780274)
XLA Ops:
  0.6 82.5 %block.1 = (bf16[6,160,256]{2,1,0:T(8,128)(2,1)}, f32[2,9,8,256]{3,2,1,0:T(8,128)}, f32[4,8,256]{2,1,0:T(8,128)}) custom-call(bf16[6,160,256]{2,1,0:T(8,128)(2,1)} %bitcast.5, bf16[60,16,256]{2,1,0:T(8,128)(2,1)} %bitcast.6, bf16[2,2304,256]{2,1,0:T(8,128)(2,1)} %bitcast.4, bf16[4,256,256]{2,1,0:T(8,128)(2,1)} %aw_hbm.1), custom_call_target="tpu_custom_call" | custom-call | tf_op jit(solution)/shard_map/block/pallas_call | solution.py:732
  83.2 1.9 %hand_on.1 = (bf16[6,160,256]{2,1,0:T(8,128)(2,1)}, f32[2,9,8,256]{3,2,1,0:T(8,128)}, f32[4,8,256]{2,1,0:T(8,128)}) custom-call(bf16[6,160,256]{2,1,0:T(8,128)(2,1)} %get-tuple-element.9.a, f32[2,9,8,256]{3,2,1,0:T(8,128)} %get-tuple-element.10.b, f32[4,8,256]{2,1,0:T(8,128)} %get-tuple-element.11.c), custom_call_target="tpu_custom_call" | custom-call | tf_op jit(solution)/shard_map/hand_on/pallas_call | solution.py:773
